TPU v7x, 1024 devices: a whole 8x8x8 slice. The times are simulated.
1024 devices in a mesh: grp: 8 (over x_lo, core), gx: 8 (over y), gy: 16 (over x_hi, z).
Axes of the slice: x: 8 (x_hi: 2, x_lo: 4; x = x_hi * 4 + x_lo), y: 8, z: 8, core: 2. Of those that a mesh axis runs over, the one named last changes fastest.
Arguments:
- state: float32 [3, 32, 512, 1024], P(None, 'grp', 'gy', 'gx'), may hold values from -6 to 6
- coefs: float32 [2, 32, 512, 1024], P(None, 'grp', 'gy', 'gx'), may hold values from 0.1 to 0.4
- lagged_absorbers: bfloat16 [7, 32, 512, 1024], P(None, 'grp', 'gy', 'gx'), may hold values from 0.049804688 to 1
- sun_route: int32 [512, 8], P('gy', 'gx'), may hold values from 0 to 16, as said below
- band_coef: bfloat16 [112, 7], replicated, may hold values from 0.0019989014 to 0.29882812
- solar: float32 [112], replicated, may hold values from 0.01 to 0.15
- layer_mass: float32 [32], replicated, may hold values from 0.5 to 2
- remap_index: int32 [32, 4], replicated, may hold values from 0 to 31, as said below
- remap_weight: float32 [32, 4], replicated, may hold values from 0.05 to 0.45
Outputs:
- new_state: float32 [3, 32, 512, 1024], P(None, 'grp', 'gy', 'gx')
- heating: float32 [32, 512, 1024], P('grp', 'gy', 'gx')
Inputs may be any that keep to these rules, and one draw needn't show every extreme that they name: `sun_route`: the block of 128 columns in face row x and gx index y is sunlit where the value is below 16; the value then names one of the 16 radiation devices of the gy index that holds row x, counted with gx fastest over the last quarter of grp; the value 16 marks a dark block. Within the 32 rows of one gy index and one gx index at most 2 blocks name the same device, and in every draw some device is named by 2 blocks of every gx index of its gy index. `remap_index`: every entry lies within 2 levels of its row's level k; the first two taps are max(k - 2, 0) and min(k + 2, 31).
All inputs are finite; a program needn't handle non-finite values.
Results may differ from a plain program's by a relative error of at most 0.0003.
Values may be sent and summed in bfloat16 or wider, within the bound.
A program may use at most 32 MiB of HBM per device.

v0:
```python
import jax
import jax.numpy as jnp
from jax import lax
from jax.sharding import PartitionSpec as P

SUB = 8
CAP = 2
RIM = 2


def padded(cells, sides, width):
    for axis, dim in sides:
        count = lax.axis_size(axis)
        ends = count - 1
        head = lax.slice_in_dim(cells, 0, width, axis=dim)
        tail = lax.slice_in_dim(cells, cells.shape[dim] - width, cells.shape[dim], axis=dim)
        cells = jnp.concatenate(
            [
                lax.ppermute(tail, axis, [(i, (i + 1) % count) for i in range(ends)]),
                cells,
                lax.ppermute(head, axis, [((i + 1) % count, i) for i in range(ends)]),
            ],
            axis=dim,
        )
    return cells


def borders(stacked, depth):
    return padded(stacked, (("gx", 3), ("gy", 2)), depth)


def advance_flow(flow_x, flow_y, beside_all, buoyancy):
    new_x = flow_x - buoyancy * (beside_all[:, 2:, 1:-1] - beside_all[:, :-2, 1:-1])
    new_y = flow_y - buoyancy * (beside_all[:, 1:-1, 2:] - beside_all[:, 1:-1, :-2])
    return (new_x, new_y)


def advance_pressure(pressure, wide_x, wide_y, stiffness):
    return pressure - stiffness * (
        wide_x[:, 2:, 1:-1] - wide_x[:, :-2, 1:-1] + (wide_y[:, 1:-1, 2:] - wide_y[:, 1:-1, :-2])
    )


def shards(
    state,
    coefs,
    lagged_absorbers,
    sun_route,
    band_coef,
    solar,
    layer_mass,
    remap_index,
    remap_weight,
):
    groups = lax.axis_size("grp")
    column_parts = lax.axis_size("gx")
    dyn_groups = 3 * groups // 4
    radiators = groups // 4 * column_parts
    level_block = state.shape[1]
    tile_rows = state.shape[2]
    tile_cols = state.shape[3]
    gases = lagged_absorbers.shape[0]
    levels = level_block * groups
    position = lax.axis_index("grp")
    is_dyn = position < dyn_groups
    flow_x, flow_y, pressure = (state[0], state[1], state[2])
    buoyancy, stiffness = (coefs[0], coefs[1])
    for substep in range(SUB):
        beside_all = borders(pressure[None], 1)[0]
        flow_x, flow_y = advance_flow(flow_x, flow_y, beside_all, buoyancy)
        both_flows = borders(jnp.stack([flow_x, flow_y]), 1)
        pressure = advance_pressure(pressure, both_flows[0], both_flows[1], stiffness)
    stepped = jnp.stack([flow_x, flow_y, pressure])
    stepped = jnp.where(is_dyn, stepped, state)
    extended_levels = padded(stepped, (("grp", 1),), RIM)
    first_level = position * level_block
    local_index = lax.dynamic_slice_in_dim(remap_index, first_level, level_block, 0) - (
        first_level - RIM
    )
    local_weight = lax.dynamic_slice_in_dim(remap_weight, first_level, level_block, 0)
    span_levels = jnp.arange(level_block + 2 * RIM, dtype=jnp.int32)
    mixing = jnp.sum(
        local_weight[:, :, None]
        * (local_index[:, :, None] == span_levels[None, None, :]).astype(jnp.float32),
        axis=1,
    )
    new_state = jnp.einsum(
        "lm,cmxy->clxy", mixing, extended_levels, precision=lax.Precision.HIGHEST
    )
    band_wide = band_coef.astype(jnp.float32)
    level_ids = jnp.arange(levels)
    triangle = (level_ids[:, None] <= level_ids[None, :]).astype(jnp.float32)
    top_flux = jnp.sum(solar)

    def heat_block(block):
        depth_in = jnp.einsum(
            "fkn,kj->fjn", block.astype(jnp.float32), triangle, precision=lax.Precision.HIGHEST
        )
        optical = jnp.einsum("gf,fkn->gkn", band_wide, depth_in, precision=lax.Precision.HIGHEST)
        flux = jnp.einsum("g,gkn->kn", solar, jnp.exp(-optical), precision=lax.Precision.HIGHEST)
        above = jnp.concatenate([jnp.broadcast_to(top_flux, (1, flux.shape[1])), flux[:-1]], 0)
        return (above - flux) / layer_mass[:, None]

    routes = sun_route[:, 0]
    sunlit = routes < radiators
    row_ids = jnp.arange(tile_rows)
    earlier = (row_ids[None, :] < row_ids[:, None]).astype(jnp.float32)
    one_hot = (routes[:, None] == jnp.arange(radiators)[None, :]).astype(jnp.float32)
    before = jnp.dot(earlier, one_hot, precision=lax.Precision.HIGHEST)
    rank_in = jnp.sum(before * one_hot, axis=1).astype(jnp.int32)
    placing = (
        sunlit[None, None, :]
        & (routes[None, None, :] == jnp.arange(radiators)[:, None, None])
        & (rank_in[None, None, :] == jnp.arange(CAP)[None, :, None])
    )
    packed = jnp.einsum(
        "dsb,flbn->dsfln",
        placing.astype(jnp.bfloat16),
        lagged_absorbers,
        preferred_element_type=jnp.float32,
    ).astype(jnp.bfloat16)
    empty_part = jnp.zeros(
        (dyn_groups * column_parts, CAP, gases, level_block, tile_cols), jnp.bfloat16
    )
    outgoing = jnp.concatenate([empty_part, packed], 0)
    arrived = lax.all_to_all(outgoing, ("grp", "gx"), split_axis=0, concat_axis=0, tiled=True)
    columns = arrived.reshape(groups, column_parts, CAP, gases, level_block, tile_cols)
    columns = jnp.transpose(columns, (1, 2, 3, 0, 4, 5)).reshape(
        column_parts * CAP, gases, levels, tile_cols
    )

    def skip_work(blocks):
        return jnp.zeros((column_parts * CAP, levels, tile_cols), jnp.float32)

    def do_work(blocks):
        return lax.map(heat_block, blocks)

    rates = lax.cond(is_dyn, skip_work, do_work, columns)
    rates = rates.reshape(column_parts, CAP, groups, level_block, tile_cols)
    returning = jnp.transpose(rates, (2, 0, 1, 3, 4)).reshape(
        groups * column_parts, CAP, level_block, tile_cols
    )
    returned = lax.all_to_all(returning, ("grp", "gx"), split_axis=0, concat_axis=0, tiled=True)[
        dyn_groups * column_parts :
    ]
    heating = jnp.einsum(
        "dsb,dsln->lbn", placing.astype(jnp.float32), returned, precision=lax.Precision.HIGHEST
    )
    return (new_state, heating)


def solution(mesh):
    in_specs = (
        P(None, "grp", "gy", "gx"),
        P(None, "grp", "gy", "gx"),
        P(None, "grp", "gy", "gx"),
        P("gy", "gx"),
        P(),
        P(),
        P(),
        P(),
        P(),
    )
    out_specs = (P(None, "grp", "gy", "gx"), P("grp", "gy", "gx"))
    return jax.shard_map(shards, mesh=mesh, in_specs=in_specs, out_specs=out_specs, check_vma=False)
```

profile of v0, /device:TPU:15, one launch (start us, length us, event | category | flops | bytes accessed | tf_op | source)
XLA Modules:
  0.0 499.7 jit_solution(16470964504343723310)
XLA Ops:
  10.3 4.9 collective-permute-start.2
  15.2 16.6 %collective-permute-start.3 = (f32[1,4,1,130]{3,1,2,0:T(4,128)S(1)}, f32[1,4,1,130]{3,1,2,0:T(4,128)S(1)}, u32[]{:S(2)}, u32[]{:S(2)}) collective-permute-start(f32[1,4,1,130]{3,1,2,0:T(4,128)S(1)} %get-tuple-element.157), channel_id=1, source_target_pairs={{1,0},{2,1},{3,2},{4,3},{5,4},{6,5},{7,6},{8,7},{9,8},{10,9},{11,1... | collective-permute-start | bytes 6248 | tf_op jit(solution)/shard_map/ppermute | solution.py:21
  38.5 4.9 collective-permute-done.5
  45.4 9.5 %collective-permute-start.7 = (f32[2,4,1,130]{3,1,2,0:T(4,128)S(1)}, f32[2,4,1,130]{3,1,2,0:T(4,128)S(1)}, u32[]{:S(2)}, u32[]{:S(2)}) collective-permute-start(f32[2,4,1,130]{3,1,2,0:T(4,128)S(1)} %get-tuple-element.109), channel_id=1, source_target_pairs={{1,0},{2,1},{3,2},{4,3},{5,4},{6,5},{7,6},{8,7},{9,8},{10,9},{11,1... | collective-permute-start | bytes 12488 | tf_op jit(solution)/shard_map/ppermute | solution.py:21
  67.8 9.6 %collective-permute-start.11 = (f32[1,4,1,130]{3,1,2,0:T(4,128)S(1)}, f32[1,4,1,130]{3,1,2,0:T(4,128)S(1)}, u32[]{:S(2)}, u32[]{:S(2)}) collective-permute-start(f32[1,4,1,130]{3,1,2,0:T(4,128)S(1)} %get-tuple-element.155), channel_id=1, source_target_pairs={{1,0},{2,1},{3,2},{4,3},{5,4},{6,5},{7,6},{8,7},{9,8},{10,9},{11,1... | collective-permute-start | bytes 6248 | tf_op jit(solution)/shard_map/ppermute | solution.py:21
  89.7 9.6 %collective-permute-start.15 = (f32[2,4,1,130]{3,1,2,0:T(4,128)S(1)}, f32[2,4,1,130]{3,1,2,0:T(4,128)S(1)}, u32[]{:S(2)}, u32[]{:S(2)}) collective-permute-start(f32[2,4,1,130]{3,1,2,0:T(4,128)S(1)} %get-tuple-element.107), channel_id=1, source_target_pairs={{1,0},{2,1},{3,2},{4,3},{5,4},{6,5},{7,6},{8,7},{9,8},{10,9},{11,1... | collective-permute-start | bytes 12488 | tf_op jit(solution)/shard_map/ppermute | solution.py:21
  110.9 9.9 %collective-permute-start.19 = (f32[1,4,1,130]{3,1,2,0:T(4,128)S(1)}, f32[1,4,1,130]{3,1,2,0:T(4,128)S(1)}, u32[]{:S(2)}, u32[]{:S(2)}) collective-permute-start(f32[1,4,1,130]{3,1,2,0:T(4,128)S(1)} %get-tuple-element.153), channel_id=1, source_target_pairs={{1,0},{2,1},{3,2},{4,3},{5,4},{6,5},{7,6},{8,7},{9,8},{10,9},{11,1... | collective-permute-start | bytes 6248 | tf_op jit(solution)/shard_map/ppermute | solution.py:21
  133.3 9.6 %collective-permute-start.23 = (f32[2,4,1,130]{3,1,2,0:T(4,128)S(1)}, f32[2,4,1,130]{3,1,2,0:T(4,128)S(1)}, u32[]{:S(2)}, u32[]{:S(2)}) collective-permute-start(f32[2,4,1,130]{3,1,2,0:T(4,128)S(1)} %get-tuple-element.105), channel_id=1, source_target_pairs={{1,0},{2,1},{3,2},{4,3},{5,4},{6,5},{7,6},{8,7},{9,8},{10,9},{11,1... | collective-permute-start | bytes 12488 | tf_op jit(solution)/shard_map/ppermute | solution.py:21
  154.4 9.6 %collective-permute-start.27 = (f32[1,4,1,130]{3,1,2,0:T(4,128)S(1)}, f32[1,4,1,130]{3,1,2,0:T(4,128)S(1)}, u32[]{:S(2)}, u32[]{:S(2)}) collective-permute-start(f32[1,4,1,130]{3,1,2,0:T(4,128)S(1)} %get-tuple-element.151), channel_id=1, source_target_pairs={{1,0},{2,1},{3,2},{4,3},{5,4},{6,5},{7,6},{8,7},{9,8},{10,9},{11,1... | collective-permute-start | bytes 6248 | tf_op jit(solution)/shard_map/ppermute | solution.py:21
  176.1 9.6 %collective-permute-start.31 = (f32[2,4,1,130]{3,1,2,0:T(4,128)S(1)}, f32[2,4,1,130]{3,1,2,0:T(4,128)S(1)}, u32[]{:S(2)}, u32[]{:S(2)}) collective-permute-start(f32[2,4,1,130]{3,1,2,0:T(4,128)S(1)} %get-tuple-element.103), channel_id=1, source_target_pairs={{1,0},{2,1},{3,2},{4,3},{5,4},{6,5},{7,6},{8,7},{9,8},{10,9},{11,1... | collective-permute-start | bytes 12488 | tf_op jit(solution)/shard_map/ppermute | solution.py:21
  197.3 9.6 %collective-permute-start.35 = (f32[1,4,1,130]{3,1,2,0:T(4,128)S(1)}, f32[1,4,1,130]{3,1,2,0:T(4,128)S(1)}, u32[]{:S(2)}, u32[]{:S(2)}) collective-permute-start(f32[1,4,1,130]{3,1,2,0:T(4,128)S(1)} %get-tuple-element.149), channel_id=1, source_target_pairs={{1,0},{2,1},{3,2},{4,3},{5,4},{6,5},{7,6},{8,7},{9,8},{10,9},{11,1... | collective-permute-start | bytes 6248 | tf_op jit(solution)/shard_map/ppermute | solution.py:21
  219.1 9.6 %collective-permute-start.39 = (f32[2,4,1,130]{3,1,2,0:T(4,128)S(1)}, f32[2,4,1,130]{3,1,2,0:T(4,128)S(1)}, u32[]{:S(2)}, u32[]{:S(2)}) collective-permute-start(f32[2,4,1,130]{3,1,2,0:T(4,128)S(1)} %get-tuple-element.101), channel_id=1, source_target_pairs={{1,0},{2,1},{3,2},{4,3},{5,4},{6,5},{7,6},{8,7},{9,8},{10,9},{11,1... | collective-permute-start | bytes 12488 | tf_op jit(solution)/shard_map/ppermute | solution.py:21
  241.0 9.4 %collective-permute-start.43 = (f32[1,4,1,130]{3,1,2,0:T(4,128)S(1)}, f32[1,4,1,130]{3,1,2,0:T(4,128)S(1)}, u32[]{:S(2)}, u32[]{:S(2)}) collective-permute-start(f32[1,4,1,130]{3,1,2,0:T(4,128)S(1)} %get-tuple-element.147), channel_id=1, source_target_pairs={{1,0},{2,1},{3,2},{4,3},{5,4},{6,5},{7,6},{8,7},{9,8},{10,9},{11,1... | collective-permute-start | bytes 6248 | tf_op jit(solution)/shard_map/ppermute | solution.py:21
  262.7 9.6 %collective-permute-start.47 = (f32[2,4,1,130]{3,1,2,0:T(4,128)S(1)}, f32[2,4,1,130]{3,1,2,0:T(4,128)S(1)}, u32[]{:S(2)}, u32[]{:S(2)}) collective-permute-start(f32[2,4,1,130]{3,1,2,0:T(4,128)S(1)} %get-tuple-element.99), channel_id=1, source_target_pairs={{1,0},{2,1},{3,2},{4,3},{5,4},{6,5},{7,6},{8,7},{9,8},{10,9},{11,1... | collective-permute-start | bytes 12488 | tf_op jit(solution)/shard_map/ppermute | solution.py:21
  284.1 9.6 %collective-permute-start.51 = (f32[1,4,1,130]{3,1,2,0:T(4,128)S(1)}, f32[1,4,1,130]{3,1,2,0:T(4,128)S(1)}, u32[]{:S(2)}, u32[]{:S(2)}) collective-permute-start(f32[1,4,1,130]{3,1,2,0:T(4,128)S(1)} %get-tuple-element.145), channel_id=1, source_target_pairs={{1,0},{2,1},{3,2},{4,3},{5,4},{6,5},{7,6},{8,7},{9,8},{10,9},{11,1... | collective-permute-start | bytes 6248 | tf_op jit(solution)/shard_map/ppermute | solution.py:21
  305.9 9.6 %collective-permute-start.55 = (f32[2,4,1,130]{3,1,2,0:T(4,128)S(1)}, f32[2,4,1,130]{3,1,2,0:T(4,128)S(1)}, u32[]{:S(2)}, u32[]{:S(2)}) collective-permute-start(f32[2,4,1,130]{3,1,2,0:T(4,128)S(1)} %get-tuple-element.97), channel_id=1, source_target_pairs={{1,0},{2,1},{3,2},{4,3},{5,4},{6,5},{7,6},{8,7},{9,8},{10,9},{11,1... | collective-permute-start | bytes 12488 | tf_op jit(solution)/shard_map/ppermute | solution.py:21
  322.9 42.5 %all-to-all-start = ((bf16[64,2,7,4,128]{4,3,2,1,0:T(4,128)(2,1)}), bf16[64,2,7,4,128]{4,3,2,1,0:T(4,128)(2,1)S(1)}, u32[]{:S(2)}, u32[]{:S(2)}) async-start(bf16[64,2,7,4,128]{4,3,2,1,0:T(4,128)(2,1)} %concatenate.138.clone), calls=%async_computation | async-start | bytes 1835008 | tf_op jit(solution)/shard_map/all_to_all | solution.py:126
  367.4 9.9 %collective-permute-start.59 = (f32[1,4,1,130]{3,1,2,0:T(4,128)S(1)}, f32[1,4,1,130]{3,1,2,0:T(4,128)S(1)}, u32[]{:S(2)}, u32[]{:S(2)}) collective-permute-start(f32[1,4,1,130]{3,1,2,0:T(4,128)S(1)} %get-tuple-element.143), channel_id=1, source_target_pairs={{1,0},{2,1},{3,2},{4,3},{5,4},{6,5},{7,6},{8,7},{9,8},{10,9},{11,1... | collective-permute-start | bytes 6248 | tf_op jit(solution)/shard_map/ppermute | solution.py:21
  377.4 11.2 %collective-permute-done.58 = f32[1,4,1,130]{3,1,2,0:T(4,128)S(1)} collective-permute-done((f32[1,4,1,130]{3,1,2,0:T(4,128)S(1)}, f32[1,4,1,130]{3,1,2,0:T(4,128)S(1)}, u32[]{:S(2)}, u32[]{:S(2)}) %collective-permute-start.58) | collective-permute-done | bytes 2112 | tf_op jit(solution)/shard_map/ppermute | solution.py:19
  399.9 9.4 %collective-permute-start.63 = (f32[2,4,1,130]{3,1,2,0:T(4,128)S(1)}, f32[2,4,1,130]{3,1,2,0:T(4,128)S(1)}, u32[]{:S(2)}, u32[]{:S(2)}) collective-permute-start(f32[2,4,1,130]{3,1,2,0:T(4,128)S(1)} %get-tuple-element.95), channel_id=1, source_target_pairs={{1,0},{2,1},{3,2},{4,3},{5,4},{6,5},{7,6},{8,7},{9,8},{10,9},{11,1... | collective-permute-start | bytes 12488 | tf_op jit(solution)/shard_map/ppermute | solution.py:21
  411.2 60.9 %conditional.1 = (f32[16,32,128]{2,1,0:T(8,128)S(1)}) conditional(s32[]{:T(128)} %convert_element_type.25, (bf16[8,2,7,8,4,128]{5,4,3,2,1,0:T(4,128)(2,1)S(1)}, f32[112]{0:T(128)S(1)}, f32[32,32]{0,1:T(8,128)S(1)}, f32[112,7]{0,1:T(8,128)S(1)}, f32[32]{0:T(128)S(1)}) %tuple.90, () %tuple.19), branch_computations={%region_2.6_spmd, %region_6.7_spmd} | conditional | flops 55517296 | bytes 4043401 | solution.py:138
  411.9 60.2 %while.9 = (s32[]{:T(128)}, f32[16,32,128]{2,1,0:T(8,128)S(1)}, bf16[16,7,32,128]{3,2,1,0:T(8,128)(2,1)S(1)}, f32[32,32]{0,1:T(8,128)S(1)}, f32[112,7]{0,1:T(8,1...) while((s32[]{:T(128)}, f32[16,32,128]{2,1,0:T(8,128)S(1)}, ...), condition=%wide.region_5.5_spmd, body=%wide.region_4.4_spmd.sunk | while | flops 55517184 | bytes 4042857 | solution.py:136
  473.0 14.4 %all-to-all-start.1 = ((f32[64,2,4,128]{3,1,2,0:T(2,128)}), f32[64,2,4,128]{3,1,2,0:T(2,128)S(1)}, u32[]{:S(2)}, u32[]{:S(2)}) async-start(f32[64,2,4,128]{3,1,2,0:T(2,128)} %bitcast.74), calls=%async_computation.1 | async-start | bytes 524288 | tf_op jit(solution)/shard_map/all_to_all | solution.py:143
  494.0 4.8 all-to-all-done.1
  (294 shorter events, 253.9 us)
Async XLA Ops:
  10.3 22.4 %collective-permute-start.2 = (f32[1,4,1,130]{3,1,2,0:T(4,128)S(1)}, f32[1,4,1,130]{3,1,2,0:T(4,128)S(1)}, u32[]{:S(2)}, u32[]{:S(2)}) collective-permute-start(f32[1,4,1,130]{3,1,2,0:T(4,128)S(1)} %get-tuple-element.156), channel_id=1, source_target_pairs={{0,1},{1,2},{2,3},{3,4},{4,5},{5,6},{6,7},{7,8},{8,9},{9,10},{10,1... | collective-permute-start | bytes 6248 | tf_op jit(solution)/shard_map/ppermute | solution.py:19
  15.2 17.5 %collective-permute-start.3 = (f32[1,4,1,130]{3,1,2,0:T(4,128)S(1)}, f32[1,4,1,130]{3,1,2,0:T(4,128)S(1)}, u32[]{:S(2)}, u32[]{:S(2)}) collective-permute-start(f32[1,4,1,130]{3,1,2,0:T(4,128)S(1)} %get-tuple-element.157), channel_id=1, source_target_pairs={{1,0},{2,1},{3,2},{4,3},{5,4},{6,5},{7,6},{8,7},{9,8},{10,9},{11,1... | collective-permute-start | bytes 6248 | tf_op jit(solution)/shard_map/ppermute | solution.py:21
  43.4 11.4 %collective-permute-start.6 = (f32[2,4,1,130]{3,1,2,0:T(4,128)S(1)}, f32[2,4,1,130]{3,1,2,0:T(4,128)S(1)}, u32[]{:S(2)}, u32[]{:S(2)}) collective-permute-start(f32[2,4,1,130]{3,1,2,0:T(4,128)S(1)} %get-tuple-element.108), channel_id=1, source_target_pairs={{0,1},{1,2},{2,3},{3,4},{4,5},{5,6},{6,7},{7,8},{8,9},{9,10},{10,1... | collective-permute-start | bytes 12488 | tf_op jit(solution)/shard_map/ppermute | solution.py:19
  65.8 11.6 %collective-permute-start.10 = (f32[1,4,1,130]{3,1,2,0:T(4,128)S(1)}, f32[1,4,1,130]{3,1,2,0:T(4,128)S(1)}, u32[]{:S(2)}, u32[]{:S(2)}) collective-permute-start(f32[1,4,1,130]{3,1,2,0:T(4,128)S(1)} %get-tuple-element.154), channel_id=1, source_target_pairs={{0,1},{1,2},{2,3},{3,4},{4,5},{5,6},{6,7},{7,8},{8,9},{9,10},{10,1... | collective-permute-start | bytes 6248 | tf_op jit(solution)/shard_map/ppermute | solution.py:19
  87.8 11.6 %collective-permute-start.14 = (f32[2,4,1,130]{3,1,2,0:T(4,128)S(1)}, f32[2,4,1,130]{3,1,2,0:T(4,128)S(1)}, u32[]{:S(2)}, u32[]{:S(2)}) collective-permute-start(f32[2,4,1,130]{3,1,2,0:T(4,128)S(1)} %get-tuple-element.106), channel_id=1, source_target_pairs={{0,1},{1,2},{2,3},{3,4},{4,5},{5,6},{6,7},{7,8},{8,9},{9,10},{10,1... | collective-permute-start | bytes 12488 | tf_op jit(solution)/shard_map/ppermute | solution.py:19
  108.9 11.9 %collective-permute-start.18 = (f32[1,4,1,130]{3,1,2,0:T(4,128)S(1)}, f32[1,4,1,130]{3,1,2,0:T(4,128)S(1)}, u32[]{:S(2)}, u32[]{:S(2)}) collective-permute-start(f32[1,4,1,130]{3,1,2,0:T(4,128)S(1)} %get-tuple-element.152), channel_id=1, source_target_pairs={{0,1},{1,2},{2,3},{3,4},{4,5},{5,6},{6,7},{7,8},{8,9},{9,10},{10,1... | collective-permute-start | bytes 6248 | tf_op jit(solution)/shard_map/ppermute | solution.py:19
  110.9 10.7 %collective-permute-start.19 = (f32[1,4,1,130]{3,1,2,0:T(4,128)S(1)}, f32[1,4,1,130]{3,1,2,0:T(4,128)S(1)}, u32[]{:S(2)}, u32[]{:S(2)}) collective-permute-start(f32[1,4,1,130]{3,1,2,0:T(4,128)S(1)} %get-tuple-element.153), channel_id=1, source_target_pairs={{1,0},{2,1},{3,2},{4,3},{5,4},{6,5},{7,6},{8,7},{9,8},{10,9},{11,1... | collective-permute-start | bytes 6248 | tf_op jit(solution)/shard_map/ppermute | solution.py:21
  131.3 11.6 %collective-permute-start.22 = (f32[2,4,1,130]{3,1,2,0:T(4,128)S(1)}, f32[2,4,1,130]{3,1,2,0:T(4,128)S(1)}, u32[]{:S(2)}, u32[]{:S(2)}) collective-permute-start(f32[2,4,1,130]{3,1,2,0:T(4,128)S(1)} %get-tuple-element.104), channel_id=1, source_target_pairs={{0,1},{1,2},{2,3},{3,4},{4,5},{5,6},{6,7},{7,8},{8,9},{9,10},{10,1... | collective-permute-start | bytes 12488 | tf_op jit(solution)/shard_map/ppermute | solution.py:19
  152.5 11.6 %collective-permute-start.26 = (f32[1,4,1,130]{3,1,2,0:T(4,128)S(1)}, f32[1,4,1,130]{3,1,2,0:T(4,128)S(1)}, u32[]{:S(2)}, u32[]{:S(2)}) collective-permute-start(f32[1,4,1,130]{3,1,2,0:T(4,128)S(1)} %get-tuple-element.150), channel_id=1, source_target_pairs={{0,1},{1,2},{2,3},{3,4},{4,5},{5,6},{6,7},{7,8},{8,9},{9,10},{10,1... | collective-permute-start | bytes 6248 | tf_op jit(solution)/shard_map/ppermute | solution.py:19
  174.2 11.6 %collective-permute-start.30 = (f32[2,4,1,130]{3,1,2,0:T(4,128)S(1)}, f32[2,4,1,130]{3,1,2,0:T(4,128)S(1)}, u32[]{:S(2)}, u32[]{:S(2)}) collective-permute-start(f32[2,4,1,130]{3,1,2,0:T(4,128)S(1)} %get-tuple-element.102), channel_id=1, source_target_pairs={{0,1},{1,2},{2,3},{3,4},{4,5},{5,6},{6,7},{7,8},{8,9},{9,10},{10,1... | collective-permute-start | bytes 12488 | tf_op jit(solution)/shard_map/ppermute | solution.py:19
  195.3 11.6 %collective-permute-start.34 = (f32[1,4,1,130]{3,1,2,0:T(4,128)S(1)}, f32[1,4,1,130]{3,1,2,0:T(4,128)S(1)}, u32[]{:S(2)}, u32[]{:S(2)}) collective-permute-start(f32[1,4,1,130]{3,1,2,0:T(4,128)S(1)} %get-tuple-element.148), channel_id=1, source_target_pairs={{0,1},{1,2},{2,3},{3,4},{4,5},{5,6},{6,7},{7,8},{8,9},{9,10},{10,1... | collective-permute-start | bytes 6248 | tf_op jit(solution)/shard_map/ppermute | solution.py:19
  217.2 11.6 %collective-permute-start.38 = (f32[2,4,1,130]{3,1,2,0:T(4,128)S(1)}, f32[2,4,1,130]{3,1,2,0:T(4,128)S(1)}, u32[]{:S(2)}, u32[]{:S(2)}) collective-permute-start(f32[2,4,1,130]{3,1,2,0:T(4,128)S(1)} %get-tuple-element.100), channel_id=1, source_target_pairs={{0,1},{1,2},{2,3},{3,4},{4,5},{5,6},{6,7},{7,8},{8,9},{9,10},{10,1... | collective-permute-start | bytes 12488 | tf_op jit(solution)/shard_map/ppermute | solution.py:19
  239.1 11.4 %collective-permute-start.42 = (f32[1,4,1,130]{3,1,2,0:T(4,128)S(1)}, f32[1,4,1,130]{3,1,2,0:T(4,128)S(1)}, u32[]{:S(2)}, u32[]{:S(2)}) collective-permute-start(f32[1,4,1,130]{3,1,2,0:T(4,128)S(1)} %get-tuple-element.146), channel_id=1, source_target_pairs={{0,1},{1,2},{2,3},{3,4},{4,5},{5,6},{6,7},{7,8},{8,9},{9,10},{10,1... | collective-permute-start | bytes 6248 | tf_op jit(solution)/shard_map/ppermute | solution.py:19
  260.8 11.6 %collective-permute-start.46 = (f32[2,4,1,130]{3,1,2,0:T(4,128)S(1)}, f32[2,4,1,130]{3,1,2,0:T(4,128)S(1)}, u32[]{:S(2)}, u32[]{:S(2)}) collective-permute-start(f32[2,4,1,130]{3,1,2,0:T(4,128)S(1)} %get-tuple-element.98), channel_id=1, source_target_pairs={{0,1},{1,2},{2,3},{3,4},{4,5},{5,6},{6,7},{7,8},{8,9},{9,10},{10,1... | collective-permute-start | bytes 12488 | tf_op jit(solution)/shard_map/ppermute | solution.py:19
  262.7 10.4 %collective-permute-start.47 = (f32[2,4,1,130]{3,1,2,0:T(4,128)S(1)}, f32[2,4,1,130]{3,1,2,0:T(4,128)S(1)}, u32[]{:S(2)}, u32[]{:S(2)}) collective-permute-start(f32[2,4,1,130]{3,1,2,0:T(4,128)S(1)} %get-tuple-element.99), channel_id=1, source_target_pairs={{1,0},{2,1},{3,2},{4,3},{5,4},{6,5},{7,6},{8,7},{9,8},{10,9},{11,1... | collective-permute-start | bytes 12488 | tf_op jit(solution)/shard_map/ppermute | solution.py:21
  282.2 11.6 %collective-permute-start.50 = (f32[1,4,1,130]{3,1,2,0:T(4,128)S(1)}, f32[1,4,1,130]{3,1,2,0:T(4,128)S(1)}, u32[]{:S(2)}, u32[]{:S(2)}) collective-permute-start(f32[1,4,1,130]{3,1,2,0:T(4,128)S(1)} %get-tuple-element.144), channel_id=1, source_target_pairs={{0,1},{1,2},{2,3},{3,4},{4,5},{5,6},{6,7},{7,8},{8,9},{9,10},{10,1... | collective-permute-start | bytes 6248 | tf_op jit(solution)/shard_map/ppermute | solution.py:19
  304.0 11.6 %collective-permute-start.54 = (f32[2,4,1,130]{3,1,2,0:T(4,128)S(1)}, f32[2,4,1,130]{3,1,2,0:T(4,128)S(1)}, u32[]{:S(2)}, u32[]{:S(2)}) collective-permute-start(f32[2,4,1,130]{3,1,2,0:T(4,128)S(1)} %get-tuple-element.96), channel_id=1, source_target_pairs={{0,1},{1,2},{2,3},{3,4},{4,5},{5,6},{6,7},{7,8},{8,9},{9,10},{10,1... | collective-permute-start | bytes 12488 | tf_op jit(solution)/shard_map/ppermute | solution.py:19
  316.9 48.5 %collective-permute-start.56 = (f32[1,4,32,1]{3,1,2,0:T(4,128)S(1)}, f32[1,4,32,1]{3,1,2,0:T(4,128)S(1)}, u32[]{:S(2)}, u32[]{:S(2)}) collective-permute-start(f32[1,4,32,1]{3,1,2,0:T(4,128)S(1)} %get-tuple-element.178), channel_id=1, source_target_pairs={{0,16},{16,32},{32,48},{48,64},{64,80},{80,96},{96,112},{1,17},{17... | collective-permute-start | bytes 1544 | tf_op jit(solution)/shard_map/ppermute | solution.py:19
  320.0 45.4 %collective-permute-start.57 = (f32[1,4,32,1]{3,1,2,0:T(4,128)S(1)}, f32[1,4,32,1]{3,1,2,0:T(4,128)S(1)}, u32[]{:S(2)}, u32[]{:S(2)}) collective-permute-start(f32[1,4,32,1]{3,1,2,0:T(4,128)S(1)} %get-tuple-element.179), channel_id=1, source_target_pairs={{16,0},{32,16},{48,32},{64,48},{80,64},{96,80},{112,96},{17,1},{33... | collective-permute-start | bytes 1544 | tf_op jit(solution)/shard_map/ppermute | solution.py:21
  322.9 87.9 %all-to-all-start = ((bf16[64,2,7,4,128]{4,3,2,1,0:T(4,128)(2,1)}), bf16[64,2,7,4,128]{4,3,2,1,0:T(4,128)(2,1)S(1)}, u32[]{:S(2)}, u32[]{:S(2)}) async-start(bf16[64,2,7,4,128]{4,3,2,1,0:T(4,128)(2,1)} %concatenate.138.clone), calls=%async_computation | async-start | bytes 1835008 | tf_op jit(solution)/shard_map/all_to_all | solution.py:126
  365.5 23.1 %collective-permute-start.58 = (f32[1,4,1,130]{3,1,2,0:T(4,128)S(1)}, f32[1,4,1,130]{3,1,2,0:T(4,128)S(1)}, u32[]{:S(2)}, u32[]{:S(2)}) collective-permute-start(f32[1,4,1,130]{3,1,2,0:T(4,128)S(1)} %get-tuple-element.142), channel_id=1, source_target_pairs={{0,1},{1,2},{2,3},{3,4},{4,5},{5,6},{6,7},{7,8},{8,9},{9,10},{10,1... | collective-permute-start | bytes 6248 | tf_op jit(solution)/shard_map/ppermute | solution.py:19
  367.4 21.2 %collective-permute-start.59 = (f32[1,4,1,130]{3,1,2,0:T(4,128)S(1)}, f32[1,4,1,130]{3,1,2,0:T(4,128)S(1)}, u32[]{:S(2)}, u32[]{:S(2)}) collective-permute-start(f32[1,4,1,130]{3,1,2,0:T(4,128)S(1)} %get-tuple-element.143), channel_id=1, source_target_pairs={{1,0},{2,1},{3,2},{4,3},{5,4},{6,5},{7,6},{8,7},{9,8},{10,9},{11,1... | collective-permute-start | bytes 6248 | tf_op jit(solution)/shard_map/ppermute | solution.py:21
  398.0 11.6 %collective-permute-start.62 = (f32[2,4,1,130]{3,1,2,0:T(4,128)S(1)}, f32[2,4,1,130]{3,1,2,0:T(4,128)S(1)}, u32[]{:S(2)}, u32[]{:S(2)}) collective-permute-start(f32[2,4,1,130]{3,1,2,0:T(4,128)S(1)} %get-tuple-element.94), channel_id=1, source_target_pairs={{0,1},{1,2},{2,3},{3,4},{4,5},{5,6},{6,7},{7,8},{8,9},{9,10},{10,1... | collective-permute-start | bytes 12488 | tf_op jit(solution)/shard_map/ppermute | solution.py:19
  473.0 25.8 %all-to-all-start.1 = ((f32[64,2,4,128]{3,1,2,0:T(2,128)}), f32[64,2,4,128]{3,1,2,0:T(2,128)S(1)}, u32[]{:S(2)}, u32[]{:S(2)}) async-start(f32[64,2,4,128]{3,1,2,0:T(2,128)} %bitcast.74), calls=%async_computation.1 | async-start | bytes 524288 | tf_op jit(solution)/shard_map/all_to_all | solution.py:143
  (52 other events, 938.8 us)
where the time goes:
time: 502 us; the launch traced here: 500 us
  starting transfers between devices  329 us (66%)
  waiting for transfers between devices  90.2 us (18%)
  matrix products  50.4 us (10%)
  other arithmetic  21.3 us (4%)
  local copies, waits for them, and re-layouts  6.61 us (1%)
    ppermute x33, starting transfers between devices, padded(): lax.ppermute(head, axis, [((i + 1) % count, i) for i in range(ends)])  185 us
    ppermute x33, starting transfers between devices, padded(): lax.ppermute(tail, axis, [(i, (i + 1) % count) for i in range(ends)])  87.4 us
    ppermute x33, waiting for transfers between devices, padded(): lax.ppermute(head, axis, [((i + 1) % count, i) for i in range(ends)])  68.7 us
    all_to_all x1, starting transfers between devices, shards(): lax.all_to_all(outgoing, ('grp', 'gx'), split_axis=0, concat_axis=0, tile...  42.5 us
    dot_general x16, matrix products, heat_block(): jnp.einsum('gf,fkn->gkn', band_wide, depth_in, precision=lax.Precision.HI...  26 us
    dot_general x16, matrix products, heat_block(): jnp.einsum('g,gkn->kn', solar, jnp.exp(-optical), precision=lax.Precision...  19.7 us
    ppermute x33, waiting for transfers between devices, padded(): lax.ppermute(tail, axis, [(i, (i + 1) % count) for i in range(ends)])  16.6 us
    all_to_all x1, starting transfers between devices, shards(): lax.all_to_all(returning, ('grp', 'gx'), split_axis=0, concat_axis=0, til...  14.4 us
  transfers between devices with their start and end apart: 68, of which 41 were waited for; matrix products, arithmetic and copies ran while one was open for 1% of the time, Pallas kernels for 0%

commit v1 on v0

v1 whole, which is shorter than its diff:
```python
import functools

import jax
import jax.numpy as jnp
from jax import lax
from jax.experimental import pallas as pl
from jax.experimental.pallas import tpu as pltpu
from jax.sharding import PartitionSpec as P

SUB = 8
RIM = 2
H = 2 * SUB
NDARK = 16
MESH = pl.DeviceIdType.MESH
LOG2E = 1.4426950408889634


def lane_ids(rows):
    return lax.broadcasted_iota(jnp.int32, (rows, 128), 1)


def ahead(main, side, lane):
    m, s = pltpu.roll(main, 126, 1), pltpu.roll(side, 126, 1)
    keep = lane < 126
    return jnp.where(keep, m, s), jnp.where(keep, s, m)


def ahead1(main, side, lane):
    m, s = pltpu.roll(main, 127, 1), pltpu.roll(side, 127, 1)
    keep = lane < 127
    return jnp.where(keep, m, s), jnp.where(keep, s, m)


def behind(main, side, lane):
    m, s = pltpu.roll(main, 2, 1), pltpu.roll(side, 2, 1)
    keep = lane >= 2
    return jnp.where(keep, m, s), jnp.where(keep, s, m)


def substeps(p, fx, fy, b, s):
    rows = p[0].shape[0]
    lane = lane_ids(rows)

    def up(v, n):
        return tuple(pltpu.roll(a, a.shape[0] - n, 0) for a in v)

    def down(v, n):
        return tuple(pltpu.roll(a, n, 0) for a in v)

    fx, bx = up(fx, 1), up(b, 1)
    fy, by = ahead1(*fy, lane), ahead1(*b, lane)
    top = H
    for step in range(SUB):
        if step == SUB // 2:
            cut = lambda v: tuple(a[8 : rows - 8] for a in v)
            p, fx, fy, bx, by, s = cut(p), cut(fx), cut(fy), cut(bx), cut(by), cut(s)
            lane = lane_ids(rows - 16)
            top = H - 8
        px, py = up(p, 2), ahead(*p, lane)
        fx = tuple(f - c * (n - o) for f, c, n, o in zip(fx, bx, px, p))
        fy = tuple(f - c * (n - o) for f, c, n, o in zip(fy, by, py, p))
        gx, gy = down(fx, 2), behind(*fy, lane)
        p = tuple(
            o - c * ((x1 - x0) + (y1 - y0))
            for o, c, x1, x0, y1, y0 in zip(p, s, fx, gx, fy, gy)
        )
    fx = down(fx, 1)[0]
    fy0, fy1 = pltpu.roll(fy[0], 1, 1), pltpu.roll(fy[1], 1, 1)
    fy = jnp.where(lane >= 1, fy0, fy1)
    own = slice(top, top + rows - 2 * H)
    return fx[own], fy[own], p[0][own]


def kernel(
    sizes,
    state, coefs, absorbers, route, band, solar, mass, ridx, rweight,
    new_state, heating,
    tile, gas, send_r, send_l, from_l, from_r, ext, block_sum, sib, chip_sum, lower, part, rest, prefix, lhs,
    in_sem, send_sem, recv_sem,
):
    n_grp, n_gx, n_gy = sizes
    dyn_groups = 3 * n_grp // 4
    chips = n_grp // 2
    levels, rows = 4, 32
    me, gx, gy = lax.axis_index("grp"), lax.axis_index("gx"), lax.axis_index("gy")
    core, chip = lax.rem(me, 2), lax.div(me, 2)
    dyn = me < dyn_groups
    has_l, has_r = gx > 0, gx < n_gx - 1
    has_u, has_d = gy > 0, gy < n_gy - 1
    land = jnp.logical_and

    loads = [
        pltpu.make_async_copy(state, tile.at[0:3, :, H : H + rows, :], in_sem.at[0]),
        pltpu.make_async_copy(coefs, tile.at[3:5, :, H : H + rows, :], in_sem.at[1]),
        pltpu.make_async_copy(absorbers, gas, in_sem.at[2]),
    ]
    for load in loads:
        load.start()

    partners = []
    for dx, cx in ((-1, has_l), (0, None), (1, has_r)):
        for dy, cy in ((-1, has_u), (0, None), (1, has_d)):
            if dx == 0 and dy == 0:
                continue
            cond = dyn
            if cx is not None:
                cond = land(cond, cx)
            if cy is not None:
                cond = land(cond, cy)
            partners.append((cond, {"gx": gx + dx, "gy": gy + dy}))
    steps = sorted({1} | {2 * d for d in range(1, chips)})
    for d in steps:
        partners.append((me + d < n_grp, {"grp": me + d}))
        partners.append((me - d >= 0, {"grp": me - d}))
    barrier = pltpu.get_barrier_semaphore()
    count = jnp.int32(0)
    for cond, dev in partners:
        count = count + cond.astype(jnp.int32)

        @pl.when(cond)
        def _(dev=dev):
            pl.semaphore_signal(barrier, inc=1, device_id=dev, device_id_type=MESH)

    number = [0]

    def remote(src, dst, dev):
        i = number[0]
        number[0] += 1
        return pltpu.make_async_remote_copy(
            src_ref=src, dst_ref=dst, send_sem=send_sem.at[i], recv_sem=recv_sem.at[i], device_id=dev, device_id_type=MESH
        )

    def all_of(*conds):
        return functools.reduce(land, conds)

    halo = [
        (all_of(dyn, has_d), all_of(dyn, has_u), remote(tile.at[:, :, rows : rows + H], tile.at[:, :, 0:H], {"gy": gy + 1})),
        (all_of(dyn, has_u), all_of(dyn, has_d), remote(tile.at[:, :, H : 2 * H], tile.at[:, :, rows + H : rows + 2 * H], {"gy": gy - 1})),
        (all_of(dyn, has_r), all_of(dyn, has_l), remote(send_r, from_l.at[:, H : H + rows], {"gx": gx + 1})),
        (all_of(dyn, has_l), all_of(dyn, has_r), remote(send_l, from_r.at[:, H : H + rows], {"gx": gx - 1})),
        (all_of(dyn, has_r, has_d), all_of(dyn, has_l, has_u), remote(send_r.at[:, rows - H :], from_l.at[:, 0:H], {"gx": gx + 1, "gy": gy + 1})),
        (all_of(dyn, has_r, has_u), all_of(dyn, has_l, has_d), remote(send_r.at[:, 0:H], from_l.at[:, rows + H :], {"gx": gx + 1, "gy": gy - 1})),
        (all_of(dyn, has_l, has_d), all_of(dyn, has_r, has_u), remote(send_l.at[:, rows - H :], from_r.at[:, 0:H], {"gx": gx - 1, "gy": gy + 1})),
        (all_of(dyn, has_l, has_u), all_of(dyn, has_r, has_d), remote(send_l.at[:, 0:H], from_r.at[:, rows + H :], {"gx": gx - 1, "gy": gy - 1})),
    ]
    true = me >= 0
    half = rows // 2
    mine = pl.multiple_of(half * core, half)
    other = pl.multiple_of(half * (1 - core), half)
    sibling = {"grp": me + 1 - 2 * core}
    to_sib = remote(block_sum.at[:, pl.ds(other, half)], sib, sibling)
    to_chips = [
        (chip + d < chips, chip - d >= 0, remote(chip_sum, lower.at[d - 1], {"grp": me + 2 * d})) for d in range(1, chips)
    ]
    to_rest = remote(part, rest, sibling)
    remap = [
        (me > 0, me < n_grp - 1, remote(ext.at[:, RIM : 2 * RIM], ext.at[:, levels + RIM :], {"grp": me - 1})),
        (me < n_grp - 1, me > 0, remote(ext.at[:, levels : levels + RIM], ext.at[:, 0:RIM], {"grp": me + 1})),
    ]

    def start(item):
        @pl.when(item[0])
        def _():
            item[2].start()

    def wait_recv(item):
        @pl.when(item[1])
        def _():
            item[2].wait_recv()

    def wait_send(item):
        @pl.when(item[0])
        def _():
            item[2].wait_send()

    loads[0].wait()
    loads[1].wait()

    lane = lane_ids(rows)
    for q in range(3):
        right = jnp.zeros((rows, 128), jnp.float32)
        left = jnp.zeros((rows, 128), jnp.float32)
        for c in (2 * q, 2 * q + 1):
            if c > 4:
                continue
            for l in range(levels):
                t = 2 * l + c % 2
                cells = tile[c, l, H : H + rows, :]
                here = lax.div(lane, 16) == t
                shift = (16 * t + 16) % 128
                right = jnp.where(here, pltpu.roll(cells, shift, 1) if shift else cells, right)
                shift = 16 * t
                left = jnp.where(here, pltpu.roll(cells, shift, 1) if shift else cells, left)
        send_r[q] = right
        send_l[q] = left

    pl.semaphore_wait(barrier, count)
    for item in halo:
        start(item)

    loads[2].wait()
    for f in range(gas.shape[0]):
        total = gas[f, 0].astype(jnp.float32)
        for l in range(1, levels):
            total = total + gas[f, l].astype(jnp.float32)
        block_sum[f] = total
    to_sib.start()

    def fill(cond, ref, *index):
        @pl.when(cond)
        def _():
            view = ref.at[index] if index else ref
            view[...] = jnp.zeros(view.shape, view.dtype)

    fill(~has_u, tile, slice(None), slice(None), slice(0, H))
    fill(~has_d, tile, slice(None), slice(None), slice(rows + H, rows + 2 * H))
    fill(~has_l, from_l)
    fill(~has_r, from_r)
    fill(land(has_l, ~has_u), from_l, slice(None), slice(0, H))
    fill(land(has_l, ~has_d), from_l, slice(None), slice(rows + H, rows + 2 * H))
    fill(land(has_r, ~has_u), from_r, slice(None), slice(0, H))
    fill(land(has_r, ~has_d), from_r, slice(None), slice(rows + H, rows + 2 * H))
    fill(me == 0, ext, slice(None), slice(0, RIM))
    fill(me == n_grp - 1, ext, slice(None), slice(levels + RIM, levels + 2 * RIM))
    for d in range(1, chips):
        fill(chip - d < 0, lower, d - 1)

    @pl.when(~dyn)
    def _():
        for c in range(3):
            ext[c, RIM : RIM + levels] = tile[c, :, H : H + rows, :]

    gpoints, gases = band.shape
    r0 = lax.broadcasted_iota(jnp.int32, (gpoints, gpoints), 0)
    r1 = lax.broadcasted_iota(jnp.int32, (gpoints, gpoints), 1)
    column = jnp.sum(jnp.where(r0 == r1, jnp.broadcast_to(solar[...], (gpoints, gpoints)), 0.0), axis=1, keepdims=True)
    logs = jnp.log2(column)
    high = logs.astype(jnp.bfloat16).astype(jnp.float32)
    middle = (logs - high).astype(jnp.bfloat16).astype(jnp.float32)
    low = logs - high - middle
    srcs = jnp.concatenate([band[...].astype(jnp.float32), high, middle, low], axis=1).astype(jnp.bfloat16)
    n_src = gases + 3
    spread0 = lax.div(lax.broadcasted_iota(jnp.int32, (8 * gpoints, gpoints), 0), 8)
    spread1 = lax.broadcasted_iota(jnp.int32, (8 * gpoints, gpoints), 1)
    spread = (spread0 == spread1).astype(jnp.float32).astype(jnp.bfloat16)
    tall = jnp.dot(spread, srcs, preferred_element_type=jnp.float32).astype(jnp.bfloat16)
    w0 = lax.broadcasted_iota(jnp.int32, (n_src, 128), 0)
    w1 = lax.broadcasted_iota(jnp.int32, (n_src, 128), 1)
    in_gas = w1 < 16 * gases
    owner = jnp.where(in_gas, lax.rem(lax.div(w1, 8), gases), w1 - 16 * gases + gases)
    widen = (w0 == owner).astype(jnp.float32).astype(jnp.bfloat16)
    wide = jnp.dot(tall, widen, preferred_element_type=jnp.float32)
    m0 = lax.broadcasted_iota(jnp.int32, (8 * gpoints, 128), 0)
    m1 = lax.broadcasted_iota(jnp.int32, (8 * gpoints, 128), 1)
    keep = (m1 >= 16 * gases) | (lax.rem(m0, 8) == lax.rem(m1, 8))
    lhs[...] = jnp.where(keep, wide, 0.0).astype(jnp.bfloat16)

    to_sib.wait_recv()
    chip_sum[...] = block_sum[:, pl.ds(mine, half), :] + sib[...]
    for item in to_chips:
        start(item)

    for item in halo:
        wait_recv(item)

    @pl.when(dyn)
    def _():
        lane_w = lane_ids(rows + 2 * H)

        def level(i, carry):
            l = lax.rem(i + 2 * core, levels)

            def pair(c):
                t = 2 * l + c % 2
                left = pltpu.roll(from_l[c // 2], lax.rem(112 - 16 * t + 128, 128), 1)
                right = pltpu.roll(from_r[c // 2], lax.rem(128 - 16 * t, 128), 1)
                side = jnp.where(lane_w < 16, right, jnp.where(lane_w >= 112, left, 0.0))
                return tile[c, l], side

            out = substeps(pair(2), pair(0), pair(1), pair(3), pair(4))
            for c in range(3):
                ext[c, RIM + l] = out[c]
            return carry

        lax.fori_loop(0, levels, level, 0)

    for item in remap:
        start(item)

    for item in to_chips:
        wait_recv(item)
    above = lower[0]
    for d in range(2, chips):
        above = above + lower[d - 1]
    even = (core == 0).astype(jnp.float32)
    part[...] = above + even * block_sum[:, pl.ds(mine, half), :]
    to_rest.start()
    prefix[...] = above + (1.0 - even) * sib[...]

    def radiate(start_row, ref):
        columns = []
        for g in range(half // 8):
            depth = ref[:, 8 * g : 8 * g + 8, :]
            for l in range(levels + 1):
                if l:
                    cells = gas[:, l - 1, pl.ds(start_row, half), :].astype(jnp.float32)
                    depth = depth + cells[:, 8 * g : 8 * g + 8, :]
                scaled = (depth * -LOG2E).reshape(8 * gases, 128)
                high = scaled.astype(jnp.bfloat16).astype(jnp.float32)
                stack = jnp.concatenate([high, scaled - high, jnp.ones((128 - 16 * gases, 128), jnp.float32)], axis=0)
                columns.append(stack.astype(jnp.bfloat16))
        cols = jnp.concatenate(columns, axis=1)
        expo = jnp.dot(lhs[...], cols, preferred_element_type=jnp.float32)
        flux = jnp.sum(jnp.exp2(expo).reshape(gpoints, 8, cols.shape[1]), axis=0)
        for l in range(levels):
            parts = []
            for g in range(half // 8):
                at = 128 * (g * (levels + 1) + l)
                parts.append(flux[:, at : at + 128] - flux[:, at + 128 : at + 256])
            diff = jnp.concatenate(parts, axis=0)
            lit = jnp.broadcast_to(route[pl.ds(start_row, half), :], (half, 128)) < NDARK
            rate = diff / jnp.full((half, 128), mass[levels * me + l])
            heating[l, pl.ds(start_row, half), :] = jnp.where(lit, rate, 0.0)

    radiate(mine, prefix)
    to_rest.wait_recv()
    radiate(other, rest)

    for item in remap:
        wait_recv(item)
    for kl in range(levels):
        k = levels * me + kl
        weights = []
        for o in range(-RIM, RIM + 1):
            w = jnp.float32(0)
            for j in range(ridx.shape[1]):
                w = w + jnp.where(ridx[k, j] == k + o, rweight[k, j], jnp.float32(0))
            weights.append(w)
        for c in range(3):
            acc = weights[0] * ext[c, kl]
            for o in range(1, 2 * RIM + 1):
                acc = acc + weights[o] * ext[c, kl + o]
            new_state[c, kl] = acc

    for item in halo + to_chips + remap:
        wait_send(item)
    to_sib.wait_send()
    to_rest.wait_send()


def shards(state, coefs, lagged_absorbers, sun_route, band_coef, solar, layer_mass, remap_index, remap_weight):
    sizes = tuple(lax.axis_size(a) for a in ("grp", "gx", "gy"))
    chips = sizes[0] // 2
    gases = lagged_absorbers.shape[0]
    levels, rows = state.shape[1:3]
    vm = lambda: pl.BlockSpec(memory_space=pltpu.VMEM)
    sm = lambda: pl.BlockSpec(memory_space=pltpu.SMEM)
    hbm = lambda: pl.BlockSpec(memory_space=pl.ANY)
    f32, bf16 = jnp.float32, jnp.bfloat16
    n_copies = 8 + 1 + (chips - 1) + 1 + 2
    return pl.pallas_call(
        functools.partial(kernel, sizes),
        out_shape=(jax.ShapeDtypeStruct(state.shape, f32), jax.ShapeDtypeStruct(state.shape[1:], f32)),
        in_specs=[hbm(), hbm(), hbm(), vm(), vm(), vm(), sm(), sm(), sm()],
        out_specs=(vm(), vm()),
        scratch_shapes=[
            pltpu.VMEM((5, levels, rows + 2 * H, 128), f32),
            pltpu.VMEM(lagged_absorbers.shape, bf16),
            pltpu.VMEM((3, rows, 128), f32),
            pltpu.VMEM((3, rows, 128), f32),
            pltpu.VMEM((3, rows + 2 * H, 128), f32),
            pltpu.VMEM((3, rows + 2 * H, 128), f32),
            pltpu.VMEM((3, levels + 2 * RIM, rows, 128), f32),
            pltpu.VMEM((gases, rows, 128), f32),
            pltpu.VMEM((gases, rows // 2, 128), f32),
            pltpu.VMEM((gases, rows // 2, 128), f32),
            pltpu.VMEM((chips - 1, gases, rows // 2, 128), f32),
            pltpu.VMEM((gases, rows // 2, 128), f32),
            pltpu.VMEM((gases, rows // 2, 128), f32),
            pltpu.VMEM((gases, rows // 2, 128), f32),
            pltpu.VMEM((8 * band_coef.shape[0], 128), bf16),
            pltpu.SemaphoreType.DMA((3,)),
            pltpu.SemaphoreType.DMA((n_copies,)),
            pltpu.SemaphoreType.DMA((n_copies,)),
        ],
        compiler_params=pltpu.CompilerParams(collective_id=0, has_side_effects=True, vmem_limit_bytes=40 * 2**20),
    )(
        state, coefs, lagged_absorbers, sun_route, band_coef, solar.reshape(1, -1), layer_mass, remap_index, remap_weight,
    )


def solution(mesh):
    tiles = P(None, "grp", "gy", "gx")
    in_specs = (tiles, tiles, tiles, P("gy", "gx"), P(), P(), P(), P(), P())
    out_specs = (tiles, P("grp", "gy", "gx"))
    return jax.shard_map(shards, mesh=mesh, in_specs=in_specs, out_specs=out_specs, check_vma=False)
```

time: 502 us -> 53.5 us (0.11)
  the two profiles are of different devices: /device:TPU:15 before, /device:TPU:59 now
where the time goes in v1:
time: 53.5 us; the launch traced here: 53.2 us
  Pallas kernels  45.1 us (84%)
  local copies, waits for them, and re-layouts  7.44 us (14%)
  between operations  0.66 us (1%)
    pallas_call x1, Pallas kernels, shards(): pl.pallas_call(functools.partial(kernel, sizes), out_shape=(jax.ShapeDtyp...  45.1 us
    unnamed x24, local copies, waits for them, and re-layouts  7.44 us

profile of v1, /device:TPU:59, one launch (start us, length us, event | category | flops | bytes accessed | tf_op | source)
XLA Modules:
  0.0 53.2 jit_solution(4481239035724265197)
XLA Ops:
  0.6 0.0 copy-start.8
  0.6 0.6 %copy-done.8 = s32[32,1]{0,1:T(1,128)S(1)} copy-done((s32[32,1]{0,1:T(1,128)S(1)}, s32[32,1]{0,1:T(1,128)}, u32[]{:S(2)}) %copy-start.8) | copy-done | bytes 152
  1.3 0.0 copy-start.5
  1.3 0.1 copy.11.route
  1.4 0.6 %copy-done.5 = s32[32,4]{0,1:T(4,128)S(1)} copy-done((s32[32,4]{0,1:T(4,128)S(1)}, s32[32,4]{0,1:T(4,128)}, u32[]{:S(2)}) %copy-start.5) | copy-done | bytes 536
  2.0 0.0 copy-start.6
  2.0 0.1 copy.13.ridx
  2.1 0.6 %copy-done.6 = f32[32,4]{0,1:T(4,128)S(1)} copy-done((f32[32,4]{0,1:T(4,128)S(1)}, f32[32,4]{0,1:T(4,128)}, u32[]{:S(2)}) %copy-start.6) | copy-done | bytes 536
  2.7 0.0 copy-start.7
  2.7 0.1 copy.14.rweight
  2.7 0.6 %copy-done.7 = bf16[112,7]{0,1:T(8,128)(2,1)S(1)} copy-done((bf16[112,7]{0,1:T(8,128)(2,1)S(1)}, bf16[112,7]{0,1:T(8,128)(2,1)}, u32[]{:S(2)}) %copy-start.7) | copy-done | bytes 1592
  3.3 0.0 copy-start.3
  3.3 0.0 copy-start.4
  3.3 0.1 copy.12.band
  3.5 0.5 copy-done.3
  4.0 0.0 copy-done.4
  4.0 0.0 copy-start
  4.0 0.9 %copy-done = bf16[7,4,32,128]{3,2,1,0:T(8,128)(2,1)S(1)} copy-done((bf16[7,4,32,128]{3,2,1,0:T(8,128)(2,1)S(1)}, bf16[7,4,32,128]{3,2,1,0:T(8,128)(2,1)}, u32[]{:S(2)}) %copy-start) | copy-done | bytes 229400
  4.9 0.0 copy-start.1
  4.9 0.9 %copy-done.1 = f32[3,4,32,128]{3,2,1,0:T(8,128)S(1)} copy-done((f32[3,4,32,128]{3,2,1,0:T(8,128)S(1)}, f32[3,4,32,128]{3,2,1,0:T(8,128)}, u32[]{:S(2)}) %copy-start.1) | copy-done | bytes 196632
  5.9 0.9 %copy-done.2 = f32[2,4,32,128]{3,2,1,0:T(8,128)S(1)} copy-done((f32[2,4,32,128]{3,2,1,0:T(8,128)S(1)}, f32[2,4,32,128]{3,2,1,0:T(8,128)}, u32[]{:S(2)}) %copy-start.2) | copy-done | bytes 131096
  6.8 45.1 %shard_map.104 = (f32[3,4,32,128]{3,2,1,0:T(8,128)S(1)}, f32[4,32,128]{2,1,0:T(8,128)S(1)}) custom-call(f32[3,4,32,128]{3,2,1,0:T(8,128)S(1)} %copy-done.1, f32[2,4,32,128]{3,2,1,0:T(8,128)S(1)} %copy-done.2, bf16[7,4,32,128]{3,2,1,0:T(8,128)(2,1)S(1)} %copy-done, s32[32,1]{1,0:T(8,128)S(1)} %copy.11.route, bf16[112,7]{1,0:T(8,128)(2,1)S(1)} %copy.12.band, ...), custom_call_target="tpu_custom_call" | custom-call | tf_op jit(solution)/shard_map/pallas_call | solution.py:361
  51.9 0.7 %copy.17 = f32[3,4,32,128]{3,2,1,0:T(8,128)} copy(f32[3,4,32,128]{3,2,1,0:T(8,128)S(1)} %get-tuple-element.4) | data formatting | bytes 393216
  52.5 0.6 %copy.18 = f32[4,32,128]{2,1,0:T(8,128)} copy(f32[4,32,128]{2,1,0:T(8,128)S(1)} %get-tuple-element.5) | data formatting | bytes 131072
  (1 shorter events, 0.0 us)
Async XLA Ops:
  0.6 0.7 %copy-start.8 = (s32[32,1]{0,1:T(1,128)S(1)}, s32[32,1]{0,1:T(1,128)}, u32[]{:S(2)}) copy-start(s32[32,1]{0,1:T(1,128)} %param.12) | copy-start | bytes 388
  1.3 0.7 %copy-start.5 = (s32[32,4]{0,1:T(4,128)S(1)}, s32[32,4]{0,1:T(4,128)}, u32[]{:S(2)}) copy-start(s32[32,4]{0,1:T(4,128)} %param.16) | copy-start | bytes 1540
  2.0 0.7 %copy-start.6 = (f32[32,4]{0,1:T(4,128)S(1)}, f32[32,4]{0,1:T(4,128)}, u32[]{:S(2)}) copy-start(f32[32,4]{0,1:T(4,128)} %param.17) | copy-start | bytes 1540
  2.7 0.7 %copy-start.7 = (bf16[112,7]{0,1:T(8,128)(2,1)S(1)}, bf16[112,7]{0,1:T(8,128)(2,1)}, u32[]{:S(2)}) copy-start(bf16[112,7]{0,1:T(8,128)(2,1)} %param.13) | copy-start | bytes 4708
  3.3 0.7 %copy-start.3 = (f32[112]{0:T(128)S(1)}, f32[112]{0:T(128)}, u32[]{:S(2)}) copy-start(f32[112]{0:T(128)} %param.14) | copy-start | bytes 1348
  3.3 0.7 %copy-start.4 = (f32[32]{0:T(128)S(1)}, f32[32]{0:T(128)}, u32[]{:S(2)}) copy-start(f32[32]{0:T(128)} %mass.1) | copy-start | bytes 388
  4.0 0.9 %copy-start = (bf16[7,4,32,128]{3,2,1,0:T(8,128)(2,1)S(1)}, bf16[7,4,32,128]{3,2,1,0:T(8,128)(2,1)}, u32[]{:S(2)}) copy-start(bf16[7,4,32,128]{3,2,1,0:T(8,128)(2,1)} %absorbers.1) | copy-start | bytes 688132
  4.9 0.9 %copy-start.1 = (f32[3,4,32,128]{3,2,1,0:T(8,128)S(1)}, f32[3,4,32,128]{3,2,1,0:T(8,128)}, u32[]{:S(2)}) copy-start(f32[3,4,32,128]{3,2,1,0:T(8,128)} %state.1) | copy-start | bytes 589828
  5.9 0.9 %copy-start.2 = (f32[2,4,32,128]{3,2,1,0:T(8,128)S(1)}, f32[2,4,32,128]{3,2,1,0:T(8,128)}, u32[]{:S(2)}) copy-start(f32[2,4,32,128]{3,2,1,0:T(8,128)} %coefs.1) | copy-start | bytes 393220

commit v2 on v1

v2 whole, which is shorter than its diff:
```python
import functools

import jax
import jax.numpy as jnp
from jax import lax
from jax.experimental import pallas as pl
from jax.experimental.pallas import tpu as pltpu
from jax.sharding import PartitionSpec as P

SUB = 8
RIM = 2
H = 2 * SUB
NDARK = 16
MESH = pl.DeviceIdType.MESH
LOG2E = 1.4426950408889634


def encode(values, biggest):
    return jnp.round(values * (32700.0 * jnp.exp2(-biggest))).astype(jnp.int32).astype(jnp.int16)


def decode(codes, biggest):
    return codes.astype(jnp.int32).astype(jnp.float32) * (jnp.exp2(biggest) * (1.0 / 32700.0))


def exponent(values):
    top = jnp.max(jnp.abs(values), axis=0, keepdims=True)
    return jnp.ceil(jnp.log2(jnp.maximum(top, 1e-30)) + 1e-3)


def lane_ids(rows):
    return lax.broadcasted_iota(jnp.int32, (rows, 128), 1)


def turned(v, shift):
    lane = lax.broadcasted_iota(jnp.int32, v.shape, 2)
    same = pltpu.roll(v, shift % 128, 2)
    across = pltpu.roll(same, 4, 1)
    keep = lane >= shift if shift > 0 else lane < 128 + shift
    return jnp.where(keep, same, across)


def chunks(start, stop, size=8):
    return [(i, min(i + size, stop)) for i in range(start, stop, size)]


def substeps(wide, p, fx, fy, bx, by, st, out):
    rows = wide.shape[1] // 8

    def row(c, r):
        return wide[c, pl.ds(r, 8, stride=rows), :]

    for i, j in chunks(0, rows):
        for r in range(i, j):
            p[r] = row(2, r)
            st[r] = row(4, r)
            fy[r] = row(1, r)
            by[r] = row(3, r)
            if r > 0:
                fx[r - 1] = row(0, r)
                bx[r - 1] = by[r]
        fy[i:j] = turned(fy[i:j], -1)
        by[i:j] = turned(by[i:j], -1)
    for step in range(SUB):
        low, high = 2 * step, rows - 2 * step
        for i, j in chunks(low, high - 2):
            here = p[i:j]
            new_x = fx[i:j] - bx[i:j] * (p[i + 2 : j + 2] - here)
            fx[i:j] = new_x
            k = max(i, low + 2)
            if k >= j:
                continue
            here = p[k:j]
            new_y = fy[k:j] - by[k:j] * (turned(here, -2) - here)
            fy[k:j] = new_y
            across = new_y - turned(new_y, 2)
            p[k:j] = here - st[k:j] * ((fx[k:j] - fx[k - 2 : j - 2]) + across)
    own = rows - 2 * H
    for i, j in chunks(0, own):
        moved = turned(fy[H + i : H + j], 1)
        for r in range(i, j):
            out[0, pl.ds(r, 8, stride=own), :] = fx[H + r - 1]
            out[1, pl.ds(r, 8, stride=own), :] = moved[r - i]
            out[2, pl.ds(r, 8, stride=own), :] = p[H + r]


def kernel(
    sizes,
    state, coefs, absorbers, route_row, band_rows, solar_row, mass_row, ridx_rows, rweight_rows,
    new_state, heating,
    route, band, solar, mass, ridx, rweight,
    wide, gas, rows_out, rows_in, sides_out, sides_in, corners_out, corners_in, exps, out, near,
    p, fx, fy, bx, by, st, block_sum, sib, chip_sum, lower, part, rest, prefix, lhs, sunlit,
    tile_sem, in_sem, send_sem, recv_sem,
):
    n_grp, n_gx, n_gy = sizes
    dyn_groups = 3 * n_grp // 4
    chips = n_grp // 2
    levels, rows = 4, 32
    me, gx, gy = lax.axis_index("grp"), lax.axis_index("gx"), lax.axis_index("gy")
    core, chip = lax.rem(me, 2), lax.div(me, 2)
    dyn = me < dyn_groups
    has_l, has_r = gx > 0, gx < n_gx - 1
    has_u, has_d = gy > 0, gy < n_gy - 1
    land = jnp.logical_and

    loads = [
        pltpu.make_async_copy(absorbers, gas, in_sem.at[0]),
        pltpu.make_async_copy(band_rows, band, in_sem.at[1]),
        pltpu.make_async_copy(solar_row, solar, in_sem.at[2]),
        pltpu.make_async_copy(route_row, route, in_sem.at[3]),
        pltpu.make_async_copy(ridx_rows, ridx, in_sem.at[4]),
        pltpu.make_async_copy(rweight_rows, rweight, in_sem.at[5]),
        pltpu.make_async_copy(mass_row, mass, in_sem.at[6]),
    ]
    tall_rows = rows + 2 * H
    tiles = []
    for l in range(levels):
        at = tall_rows * l + H
        tiles.append(pltpu.make_async_copy(state.at[:, l], wide.at[0:3, at : at + rows, :], tile_sem.at[0, l]))
        tiles.append(pltpu.make_async_copy(coefs.at[:, l], wide.at[3:5, at : at + rows, :], tile_sem.at[1, l]))
    for load in tiles + loads:
        load.start()

    partners = []
    for dx, cx in ((-1, has_l), (0, None), (1, has_r)):
        for dy, cy in ((-1, has_u), (0, None), (1, has_d)):
            if dx == 0 and dy == 0:
                continue
            cond = dyn
            if cx is not None:
                cond = land(cond, cx)
            if cy is not None:
                cond = land(cond, cy)
            partners.append((cond, {"gx": gx + dx, "gy": gy + dy}))
    steps = sorted({1} | {2 * d for d in range(1, chips)})
    for d in steps:
        partners.append((me + d < n_grp, {"grp": me + d}))
        partners.append((me - d >= 0, {"grp": me - d}))
    barrier = pltpu.get_barrier_semaphore()
    count = jnp.int32(0)
    for cond, dev in partners:
        count = count + cond.astype(jnp.int32)

        @pl.when(cond)
        def _(dev=dev):
            pl.semaphore_signal(barrier, inc=1, device_id=dev, device_id_type=MESH)

    number = [0]

    def remote(src, dst, dev):
        i = number[0]
        number[0] += 1
        return pltpu.make_async_remote_copy(
            src_ref=src, dst_ref=dst, send_sem=send_sem.at[i], recv_sem=recv_sem.at[i], device_id=dev, device_id_type=MESH
        )

    def all_of(*conds):
        return functools.reduce(land, conds)

    halo = [
        (all_of(dyn, has_d), all_of(dyn, has_u), remote(rows_out.at[:, rows - H :], rows_in.at[0], {"gy": gy + 1})),
        (all_of(dyn, has_u), all_of(dyn, has_d), remote(rows_out.at[:, 0:H], rows_in.at[1], {"gy": gy - 1})),
        (all_of(dyn, has_r), all_of(dyn, has_l), remote(sides_out.at[0], sides_in.at[0], {"gx": gx + 1})),
        (all_of(dyn, has_l), all_of(dyn, has_r), remote(sides_out.at[1], sides_in.at[1], {"gx": gx - 1})),
    ]
    for side, (to, back, dx) in enumerate(((has_r, has_l, 1), (has_l, has_r, -1))):
        bottom = corners_out.at[side, :, rows - H :]
        top = corners_out.at[side, :, 0:H]
        halo += [
            (all_of(dyn, to, has_d), all_of(dyn, back, has_u), remote(bottom, corners_in.at[side, 0], {"gx": gx + dx, "gy": gy + 1})),
            (all_of(dyn, to, has_u), all_of(dyn, back, has_d), remote(top, corners_in.at[side, 1], {"gx": gx + dx, "gy": gy - 1})),
        ]
    half = rows // 2
    mine = pl.multiple_of(half * core, half)
    other = pl.multiple_of(half * (1 - core), half)
    sibling = {"grp": me + 1 - 2 * core}
    to_sib = remote(block_sum.at[:, pl.ds(other, half)], sib, sibling)
    to_chips = [
        (chip + d < chips, chip - d >= 0, remote(chip_sum, lower.at[d - 1], {"grp": me + 2 * d})) for d in range(1, chips)
    ]
    to_rest = remote(part, rest, sibling)
    remap = [
        (me > 0, me < n_grp - 1, remote(out.at[:, 0 : RIM * rows], near.at[1], {"grp": me - 1})),
        (me < n_grp - 1, me > 0, remote(out.at[:, (levels - RIM) * rows : levels * rows], near.at[0], {"grp": me + 1})),
    ]

    def start(item):
        @pl.when(item[0])
        def _():
            item[2].start()

    def wait_recv(item):
        @pl.when(item[1])
        def _():
            item[2].wait_recv()

    def wait_send(item):
        @pl.when(item[0])
        def _():
            item[2].wait_send()

    for load in tiles:
        load.wait()

    lane = lane_ids(rows)
    exps[...] = jnp.zeros(exps.shape, jnp.float32)
    for q in range(3):
        right = jnp.zeros((rows, 128), jnp.float32)
        left = jnp.zeros((rows, 128), jnp.float32)
        for c in (2 * q, 2 * q + 1):
            if c > 4:
                continue
            for l in range(levels):
                t = 2 * l + c % 2
                cells = wide[c, tall_rows * l + H : tall_rows * l + H + rows, :]
                biggest = exponent(cells)
                exps[levels * c + l : levels * c + l + 1, :] = biggest
                rows_out[levels * c + l] = encode(cells, biggest)
                here = lax.div(lane, 16) == t
                shift = (16 * t + 16) % 128
                right = jnp.where(here, pltpu.roll(cells, shift, 1) if shift else cells, right)
                shift = 16 * t
                left = jnp.where(here, pltpu.roll(cells, shift, 1) if shift else cells, left)
        for side, strip in enumerate((right, left)):
            biggest = exponent(strip)
            sides_out[side, q, 0:rows] = encode(strip, biggest)
            sides_out[side, q, rows : rows + 16] = jnp.broadcast_to(biggest, (16, 128)).astype(jnp.int32).astype(jnp.int16)
            corners_out[side, q] = strip.astype(jnp.bfloat16)
    for i in range(2):
        held = exps[16 * i : 16 * i + 16, :]
        rows_out[20 + i] = jnp.concatenate([held, held], axis=0).astype(jnp.int32).astype(jnp.int16)

    pl.semaphore_wait(barrier, count)
    for item in halo:
        start(item)

    loads[0].wait()
    for f in range(gas.shape[0]):
        total = gas[f, 0].astype(jnp.float32)
        for l in range(1, levels):
            total = total + gas[f, l].astype(jnp.float32)
        block_sum[f] = total
    to_sib.start()

    def fill(cond, ref, *index, value=0):
        @pl.when(cond)
        def _():
            view = ref.at[index] if index else ref
            view[...] = jnp.full(view.shape, value, view.dtype)

    fill(~has_u, rows_in, 0)
    fill(~has_d, rows_in, 1)
    fill(~has_l, sides_in, 0)
    fill(~has_r, sides_in, 1)
    fill(~land(has_l, has_u), corners_in, 0, 0)
    fill(~land(has_l, has_d), corners_in, 0, 1)
    fill(~land(has_r, has_u), corners_in, 1, 0)
    fill(~land(has_r, has_d), corners_in, 1, 1)
    fill(me == 0, near, 0)
    fill(me == n_grp - 1, near, 1)
    for d in range(1, chips):
        fill(chip - d < 0, lower, d - 1, value=-4 * 8191)

    @pl.when(~dyn)
    def _():
        for c in range(3):
            for l in range(levels):
                out[c, rows * l : rows * l + rows, :] = wide[c, tall_rows * l + H : tall_rows * l + H + rows, :]

    for load in loads[1:]:
        load.wait()
    gases, gpoints = band.shape
    r0 = lax.broadcasted_iota(jnp.int32, (gpoints, gpoints), 0)
    r1 = lax.broadcasted_iota(jnp.int32, (gpoints, gpoints), 1)
    logs = jnp.log2(solar[...])
    high = logs.astype(jnp.bfloat16).astype(jnp.float32)
    middle = (logs - high).astype(jnp.bfloat16).astype(jnp.float32)
    low = logs - high - middle
    srcs = jnp.concatenate([band[...].astype(jnp.float32), high, middle, low], axis=0).astype(jnp.bfloat16)
    n_src = gases + 3
    l0 = lax.broadcasted_iota(jnp.int32, (rows, rows), 0)
    l1 = lax.broadcasted_iota(jnp.int32, (rows, rows), 1)
    lit_row = jnp.broadcast_to((route[...] < NDARK).astype(jnp.float32), (rows, rows))
    sunlit[...] = jnp.broadcast_to(jnp.sum(jnp.where(l0 == l1, lit_row, 0.0), axis=1, keepdims=True), (rows, 128))
    spread0 = lax.div(lax.broadcasted_iota(jnp.int32, (8 * gpoints, gpoints), 0), 8)
    spread1 = lax.broadcasted_iota(jnp.int32, (8 * gpoints, gpoints), 1)
    spread = (spread0 == spread1).astype(jnp.float32).astype(jnp.bfloat16)
    tall = lax.dot_general(spread, srcs, (((1,), (1,)), ((), ())), preferred_element_type=jnp.float32).astype(jnp.bfloat16)
    w0 = lax.broadcasted_iota(jnp.int32, (n_src, 128), 0)
    w1 = lax.broadcasted_iota(jnp.int32, (n_src, 128), 1)
    in_gas = w1 < 16 * gases
    owner = jnp.where(in_gas, lax.rem(lax.div(w1, 8), gases), w1 - 16 * gases + gases)
    widen = (w0 == owner).astype(jnp.float32).astype(jnp.bfloat16)
    spread_all = jnp.dot(tall, widen, preferred_element_type=jnp.float32)
    m0 = lax.broadcasted_iota(jnp.int32, (8 * gpoints, 128), 0)
    m1 = lax.broadcasted_iota(jnp.int32, (8 * gpoints, 128), 1)
    keep = (m1 >= 16 * gases) | (lax.rem(m0, 8) == lax.rem(m1, 8))
    lhs[...] = jnp.where(keep, spread_all, 0.0).astype(jnp.bfloat16)

    to_sib.wait_recv()
    both = block_sum[:, pl.ds(mine, half), :] + sib[...]
    chip_sum[...] = jnp.round((both - 4.0) * 8191.0).astype(jnp.int32).astype(jnp.int16)
    for item in to_chips:
        start(item)

    for item in halo:
        wait_recv(item)

    @pl.when(dyn)
    def _():
        for i, at in enumerate((0, H + rows)):
            biggest = jnp.concatenate([rows_in[i, 20], rows_in[i, 21]], axis=0).astype(jnp.int32).astype(jnp.float32)
            exps[...] = biggest
            for c in range(5):
                for l in range(levels):
                    k = levels * c + l
                    wide[c, tall_rows * l + at : tall_rows * l + at + H, :] = decode(rows_in[i, k], exps[k : k + 1, :])
        lane_w = lane_ids(rows + 2 * H)
        for q in range(3):
            strips = []
            for side in range(2):
                biggest = sides_in[side, q, rows : rows + 16].astype(jnp.int32).astype(jnp.float32)[0:1]
                middle = decode(sides_in[side, q, 0:rows], biggest)
                ends = [corners_in[side, i, q].astype(jnp.float32) for i in range(2)]
                strips.append(jnp.concatenate([ends[0], middle, ends[1]], axis=0))
            for c in (2 * q, 2 * q + 1):
                if c > 4:
                    continue
                for l in range(levels):
                    t = 2 * l + c % 2
                    shift = (112 - 16 * t) % 128
                    left = pltpu.roll(strips[0], shift, 1) if shift else strips[0]
                    shift = (128 - 16 * t) % 128
                    right = pltpu.roll(strips[1], shift, 1) if shift else strips[1]
                    wide[c, tall_rows * (levels + l) : tall_rows * (levels + l + 1), :] = jnp.where(
                        lane_w < 16, right, jnp.where(lane_w >= 112, left, 0.0)
                    )
        substeps(wide, p, fx, fy, bx, by, st, out)

    for item in remap:
        start(item)

    for item in to_chips:
        wait_recv(item)
    above = jnp.zeros(rest.shape, jnp.float32)
    for d in range(1, chips):
        above = above + (lower[d - 1].astype(jnp.int32).astype(jnp.float32) * (1.0 / 8191.0) + 4.0)
    even = (core == 0).astype(jnp.float32)
    part[...] = above + even * block_sum[:, pl.ds(mine, half), :]
    to_rest.start()
    prefix[...] = above + (1.0 - even) * sib[...]

    def radiate(start_row, ref):
        columns = []
        for g in range(half // 8):
            depth = ref[:, 8 * g : 8 * g + 8, :]
            for l in range(levels + 1):
                if l:
                    cells = gas[:, l - 1, pl.ds(start_row, half), :].astype(jnp.float32)
                    depth = depth + cells[:, 8 * g : 8 * g + 8, :]
                scaled = (depth * -LOG2E).reshape(8 * gases, 128)
                high = scaled.astype(jnp.bfloat16).astype(jnp.float32)
                stack = jnp.concatenate([high, scaled - high, jnp.ones((128 - 16 * gases, 128), jnp.float32)], axis=0)
                columns.append(stack.astype(jnp.bfloat16))
        cols = jnp.concatenate(columns, axis=1)
        expo = jnp.dot(lhs[...], cols, preferred_element_type=jnp.float32)
        flux = jnp.sum(jnp.exp2(expo).reshape(gpoints, 8, cols.shape[1]), axis=0)
        for l in range(levels):
            parts = []
            for g in range(half // 8):
                at = 128 * (g * (levels + 1) + l)
                parts.append(flux[:, at : at + 128] - flux[:, at + 128 : at + 256])
            diff = jnp.concatenate(parts, axis=0)
            lit = sunlit[pl.ds(start_row, half), :] > 0.5
            rate = diff / jnp.full((half, 128), mass[0, levels * me + l])
            heating[l, pl.ds(start_row, half), :] = jnp.where(lit, rate, 0.0)

    radiate(mine, prefix)
    to_rest.wait_recv()
    radiate(other, rest)

    for item in remap:
        wait_recv(item)
    for kl in range(levels):
        k = levels * me + kl
        weights = []
        for o in range(-RIM, RIM + 1):
            w = jnp.float32(0)
            for j in range(ridx.shape[0]):
                w = w + jnp.where(ridx[j, k] == k + o, rweight[j, k], jnp.float32(0))
            weights.append(w)
        for c in range(3):
            acc = jnp.zeros((rows, 128), jnp.float32)
            for o in range(-RIM, RIM + 1):
                m = kl + o
                ref, m = (near.at[0], m + RIM) if m < 0 else (out, m) if m < levels else (near.at[1], m - levels)
                cells = ref[c, rows * m : rows * m + rows, :]
                acc = acc + weights[o + RIM] * cells
            new_state[c, kl] = acc

    for item in halo + to_chips + remap:
        wait_send(item)
    to_sib.wait_send()
    to_rest.wait_send()


def shards(state, coefs, lagged_absorbers, sun_route, band_coef, solar, layer_mass, remap_index, remap_weight):
    sizes = tuple(lax.axis_size(a) for a in ("grp", "gx", "gy"))
    chips = sizes[0] // 2
    gases = lagged_absorbers.shape[0]
    levels, rows = state.shape[1:3]
    f32, bf16, i16 = jnp.float32, jnp.bfloat16, jnp.int16
    operands = (
        state, coefs, lagged_absorbers, sun_route.T, band_coef.T, solar.reshape(1, -1), layer_mass.reshape(1, -1),
        remap_index.T, remap_weight.T,
    )
    n_copies = 8 + 1 + (chips - 1) + 1 + 2
    return pl.pallas_call(
        functools.partial(kernel, sizes),
        out_shape=(jax.ShapeDtypeStruct(state.shape, f32), jax.ShapeDtypeStruct(state.shape[1:], f32)),
        in_specs=[pl.BlockSpec(memory_space=pltpu.HBM)] * len(operands),
        out_specs=(pl.BlockSpec(memory_space=pltpu.VMEM),) * 2,
        scratch_shapes=[
            pltpu.VMEM((1, rows), jnp.int32),
            pltpu.VMEM(band_coef.shape[::-1], bf16),
            pltpu.VMEM((1, solar.shape[0]), f32),
            pltpu.SMEM((1, layer_mass.shape[0]), f32),
            pltpu.SMEM(remap_index.shape[::-1], jnp.int32),
            pltpu.SMEM(remap_weight.shape[::-1], f32),
            pltpu.VMEM((5, 2 * levels * (rows + 2 * H), 128), f32),
            pltpu.VMEM(lagged_absorbers.shape, bf16),
            pltpu.VMEM((22, rows, 128), i16),
            pltpu.VMEM((2, 22, H, 128), i16),
            pltpu.VMEM((2, 3, rows + 16, 128), i16),
            pltpu.VMEM((2, 3, rows + 16, 128), i16),
            pltpu.VMEM((2, 3, rows, 128), bf16),
            pltpu.VMEM((2, 2, 3, H, 128), bf16),
            pltpu.VMEM((32, 128), f32),
            pltpu.VMEM((3, 2 * levels * rows, 128), f32),
            pltpu.VMEM((2, 3, RIM * rows, 128), f32),
            *[pltpu.VMEM((rows + 2 * H, 2 * levels, 128), f32)] * 6,
            pltpu.VMEM((gases, rows, 128), f32),
            pltpu.VMEM((gases, rows // 2, 128), f32),
            pltpu.VMEM((gases, rows // 2, 128), i16),
            pltpu.VMEM((chips - 1, gases, rows // 2, 128), i16),
            pltpu.VMEM((gases, rows // 2, 128), f32),
            pltpu.VMEM((gases, rows // 2, 128), f32),
            pltpu.VMEM((gases, rows // 2, 128), f32),
            pltpu.VMEM((8 * band_coef.shape[0], 128), bf16),
            pltpu.VMEM((rows, 128), f32),
            pltpu.SemaphoreType.DMA((2, levels)),
            pltpu.SemaphoreType.DMA((7,)),
            pltpu.SemaphoreType.DMA((n_copies,)),
            pltpu.SemaphoreType.DMA((n_copies,)),
        ],
        compiler_params=pltpu.CompilerParams(collective_id=0, has_side_effects=True, vmem_limit_bytes=40 * 2**20),
    )(
        *[pltpu.with_memory_space_constraint(a, pltpu.HBM) for a in operands]
    )


def solution(mesh):
    tiles = P(None, "grp", "gy", "gx")
    in_specs = (tiles, tiles, tiles, P("gy", "gx"), P(), P(), P(), P(), P())
    out_specs = (tiles, P("grp", "gy", "gx"))
    return jax.shard_map(shards, mesh=mesh, in_specs=in_specs, out_specs=out_specs, check_vma=False)
```

time: 53.5 us -> 39.2 us (0.73)
  Pallas kernels: 45.1 us -> 37.1 us
  local copies, waits for them, and re-layouts: 7.44 us -> 1.31 us
    pallas_call x1, Pallas kernels: 45.1 us -> 37.1 us  [shards(): pl.pallas_call(functools.partial(kernel, sizes), out_shape=(jax.ShapeDtyp...]
    unnamed x24 -> x2, local copies, waits for them, and re-layouts: 7.44 us -> 1.31 us
where the time goes in v2:
time: 39.2 us; the launch traced here: 39 us
  Pallas kernels  37.1 us (95%)
  local copies, waits for them, and re-layouts  1.31 us (3%)
  between operations  0.64 us (2%)
    pallas_call x1, Pallas kernels, shards(): pl.pallas_call(functools.partial(kernel, sizes), out_shape=(jax.ShapeDtyp...  37.1 us
    unnamed x2, local copies, waits for them, and re-layouts  1.31 us

profile of v2, /device:TPU:59, one launch (start us, length us, event | category | flops | bytes accessed | tf_op | source)
XLA Modules:
  0.0 39.0 jit_solution(7966913001444598393)
XLA Ops:
  0.6 37.1 %shard_map.104 = (f32[3,4,32,128]{3,2,1,0:T(8,128)S(1)}, f32[4,32,128]{2,1,0:T(8,128)S(1)}) custom-call(f32[3,4,32,128]{3,2,1,0:T(8,128)} %state.1, f32[2,4,32,128]{3,2,1,0:T(8,128)} %coefs.1, bf16[7,4,32,128]{3,2,1,0:T(8,128)(2,1)} %absorbers.1, s32[1,32]{1,0:T(1,128)} %bitcast.9, bf16[7,112]{1,0:T(8,128)(2,1)} %bitcast.6, f32[1,112]{1,0:T(1,128)} %bitcast.10, ...), custom_call_target="tpu_custom_call" | custom-call | tf_op jit(solution)/shard_map/pallas_call | solution.py:419
  37.7 0.7 %copy.13 = f32[3,4,32,128]{3,2,1,0:T(8,128)} copy(f32[3,4,32,128]{3,2,1,0:T(8,128)S(1)} %get-tuple-element.4) | data formatting | bytes 393216
  38.4 0.6 %copy.14 = f32[4,32,128]{2,1,0:T(8,128)} copy(f32[4,32,128]{2,1,0:T(8,128)S(1)} %get-tuple-element.5) | data formatting | bytes 131072

commit v3 on v2

--- a/solution.py
+++ b/solution.py
@@ -11,6 +11,8 @@
 RIM = 2
 H = 2 * SUB
 NDARK = 16
+PLANES = 22
+DIRECT = 14
 MESH = pl.DeviceIdType.MESH
 LOG2E = 1.4426950408889634
 
@@ -61,27 +63,24 @@
                 bx[r - 1] = by[r]
         fy[i:j] = turned(fy[i:j], -1)
         by[i:j] = turned(by[i:j], -1)
+    first = 0
+    pv, xv, yv = p[...], fx[0 : rows - 1], fy[...]
     for step in range(SUB):
-        low, high = 2 * step, rows - 2 * step
-        for i, j in chunks(low, high - 2):
-            here = p[i:j]
-            new_x = fx[i:j] - bx[i:j] * (p[i + 2 : j + 2] - here)
-            fx[i:j] = new_x
-            k = max(i, low + 2)
-            if k >= j:
-                continue
-            here = p[k:j]
-            new_y = fy[k:j] - by[k:j] * (turned(here, -2) - here)
-            fy[k:j] = new_y
-            across = new_y - turned(new_y, 2)
-            p[k:j] = here - st[k:j] * ((fx[k:j] - fx[k - 2 : j - 2]) + across)
+        n = rows - 2 * first
+        xv = xv[0 : n - 2] - bx[first : first + n - 2] * (pv[2:n] - pv[0 : n - 2])
+        here = pv[2 : n - 2]
+        inner = slice(first + 2, first + n - 2)
+        yv = yv[2 : n - 2] - by[inner] * (turned(here, -2) - here)
+        across = yv - turned(yv, 2)
+        pv = here - st[inner] * ((xv[2 : n - 2] - xv[0 : n - 4]) + across)
+        last, xv = xv, xv[2 : n - 2]
+        first += 2
     own = rows - 2 * H
-    for i, j in chunks(0, own):
-        moved = turned(fy[H + i : H + j], 1)
-        for r in range(i, j):
-            out[0, pl.ds(r, 8, stride=own), :] = fx[H + r - 1]
-            out[1, pl.ds(r, 8, stride=own), :] = moved[r - i]
-            out[2, pl.ds(r, 8, stride=own), :] = p[H + r]
+    moved = turned(yv, 1)
+    for r in range(own):
+        out[0, pl.ds(r, 8, stride=own), :] = last[r + 1]
+        out[1, pl.ds(r, 8, stride=own), :] = moved[r]
+        out[2, pl.ds(r, 8, stride=own), :] = pv[r]
 
 
 def kernel(
@@ -89,7 +88,7 @@
     state, coefs, absorbers, route_row, band_rows, solar_row, mass_row, ridx_rows, rweight_rows,
     new_state, heating,
     route, band, solar, mass, ridx, rweight,
-    wide, gas, rows_out, rows_in, sides_out, sides_in, corners_out, corners_in, exps, out, near,
+    wide, gas, rows_out, rows_in, sides_out, sides_in, corners_out, corners_in, exps, out, near, passing,
     p, fx, fy, bx, by, st, block_sum, sib, chip_sum, lower, part, rest, prefix, lhs, sunlit,
     tile_sem, in_sem, send_sem, recv_sem,
 ):
@@ -133,6 +132,12 @@
             if cy is not None:
                 cond = land(cond, cy)
             partners.append((cond, {"gx": gx + dx, "gy": gy + dy}))
+    seam = n_gy // 2
+    far = seam >= 2
+    edge_d, edge_u = land(dyn, gy == seam - 1), land(dyn, gy == seam)
+    pass_d, pass_u = land(dyn, gy == seam - 2), land(dyn, gy == seam + 1)
+    if far:
+        partners += [(pass_d, {"gy": gy + 2}), (edge_u, {"gy": gy - 2}), (pass_u, {"gy": gy - 2}), (edge_d, {"gy": gy + 2})]
     steps = sorted({1} | {2 * d for d in range(1, chips)})
     for d in steps:
         partners.append((me + d < n_grp, {"grp": me + d}))
@@ -148,19 +153,43 @@
 
     number = [0]
 
-    def remote(src, dst, dev):
+    def remote(src, dst, dev, arrival=None):
         i = number[0]
         number[0] += 1
         return pltpu.make_async_remote_copy(
-            src_ref=src, dst_ref=dst, send_sem=send_sem.at[i], recv_sem=recv_sem.at[i], device_id=dev, device_id_type=MESH
+            src_ref=src,
+            dst_ref=dst,
+            send_sem=send_sem.at[i],
+            recv_sem=recv_sem.at[i if arrival is None else arrival],
+            device_id=dev,
+            device_id_type=MESH,
         )
 
     def all_of(*conds):
         return functools.reduce(land, conds)
 
+    down, up = all_of(dyn, has_d), all_of(dyn, has_u)
     halo = [
-        (all_of(dyn, has_d), all_of(dyn, has_u), remote(rows_out.at[:, rows - H :], rows_in.at[0], {"gy": gy + 1})),
-        (all_of(dyn, has_u), all_of(dyn, has_d), remote(rows_out.at[:, 0:H], rows_in.at[1], {"gy": gy - 1})),
+        (down, up, remote(rows_out.at[0:DIRECT, rows - H :], rows_in.at[0, 0:DIRECT], {"gy": gy + 1})),
+        (up, down, remote(rows_out.at[0:DIRECT, 0:H], rows_in.at[1, 0:DIRECT], {"gy": gy - 1})),
+    ]
+    rest_down = rows_out.at[DIRECT:PLANES, rows - H :]
+    rest_up = rows_out.at[DIRECT:PLANES, 0:H]
+    down_sem, up_sem, pass_sem = number[0], number[0] + 1, number[0] + 2
+    by_down = (land(down, ~edge_d) if far else down, up, remote(rest_down, rows_in.at[0, DIRECT:PLANES], {"gy": gy + 1}))
+    by_up = (land(up, ~edge_u) if far else up, down, remote(rest_up, rows_in.at[1, DIRECT:PLANES], {"gy": gy - 1}))
+    passes = []
+    if far:
+        to_pass_d = (edge_d, pass_d, remote(rest_down, passing, {"gy": gy - 1}))
+        to_pass_u = (edge_u, pass_u, remote(rest_up, passing, {"gy": gy + 1}, pass_sem))
+        passes = [to_pass_d, to_pass_u]
+    relays = []
+    if far:
+        relays = [
+            (pass_d, None, remote(passing, rows_in.at[0, DIRECT:PLANES], {"gy": gy + 2}, down_sem)),
+            (pass_u, None, remote(passing, rows_in.at[1, DIRECT:PLANES], {"gy": gy - 2}, up_sem)),
+        ]
+    halo = halo + [by_down, by_up] + [
         (all_of(dyn, has_r), all_of(dyn, has_l), remote(sides_out.at[0], sides_in.at[0], {"gx": gx + 1})),
         (all_of(dyn, has_l), all_of(dyn, has_r), remote(sides_out.at[1], sides_in.at[1], {"gx": gx - 1})),
     ]
@@ -232,7 +261,7 @@
         rows_out[20 + i] = jnp.concatenate([held, held], axis=0).astype(jnp.int32).astype(jnp.int16)
 
     pl.semaphore_wait(barrier, count)
-    for item in halo:
+    for item in passes + halo:
         start(item)
 
     loads[0].wait()
@@ -242,6 +271,9 @@
             total = total + gas[f, l].astype(jnp.float32)
         block_sum[f] = total
     to_sib.start()
+    for item, relay in zip(passes, relays):
+        wait_recv(item)
+        start(relay)
 
     def fill(cond, ref, *index, value=0):
         @pl.when(cond)
@@ -399,7 +431,7 @@
                 acc = acc + weights[o + RIM] * cells
             new_state[c, kl] = acc
 
-    for item in halo + to_chips + remap:
+    for item in passes + relays + halo + to_chips + remap:
         wait_send(item)
     to_sib.wait_send()
     to_rest.wait_send()
@@ -415,7 +447,7 @@
         state, coefs, lagged_absorbers, sun_route.T, band_coef.T, solar.reshape(1, -1), layer_mass.reshape(1, -1),
         remap_index.T, remap_weight.T,
     )
-    n_copies = 8 + 1 + (chips - 1) + 1 + 2
+    n_copies = 14 + 1 + (chips - 1) + 1 + 2
     return pl.pallas_call(
         functools.partial(kernel, sizes),
         out_shape=(jax.ShapeDtypeStruct(state.shape, f32), jax.ShapeDtypeStruct(state.shape[1:], f32)),
@@ -430,8 +462,8 @@
             pltpu.SMEM(remap_weight.shape[::-1], f32),
             pltpu.VMEM((5, 2 * levels * (rows + 2 * H), 128), f32),
             pltpu.VMEM(lagged_absorbers.shape, bf16),
-            pltpu.VMEM((22, rows, 128), i16),
-            pltpu.VMEM((2, 22, H, 128), i16),
+            pltpu.VMEM((PLANES, rows, 128), i16),
+            pltpu.VMEM((2, PLANES, H, 128), i16),
             pltpu.VMEM((2, 3, rows + 16, 128), i16),
             pltpu.VMEM((2, 3, rows + 16, 128), i16),
             pltpu.VMEM((2, 3, rows, 128), bf16),
@@ -439,6 +471,7 @@
             pltpu.VMEM((32, 128), f32),
             pltpu.VMEM((3, 2 * levels * rows, 128), f32),
             pltpu.VMEM((2, 3, RIM * rows, 128), f32),
+            pltpu.VMEM((PLANES - DIRECT, H, 128), i16),
             *[pltpu.VMEM((rows + 2 * H, 2 * levels, 128), f32)] * 6,
             pltpu.VMEM((gases, rows, 128), f32),
             pltpu.VMEM((gases, rows // 2, 128), f32),

time: 39.2 us -> 34.8 us (0.89)
  Pallas kernels: 37.1 us -> 32.7 us
    pallas_call x1, Pallas kernels: 37.1 us -> 32.7 us  [shards(): pl.pallas_call(functools.partial(kernel, sizes), out_shape=(jax.ShapeDtyp...]
where the time goes in v3:
time: 34.8 us; the launch traced here: 34.6 us
  Pallas kernels  32.7 us (94%)
  local copies, waits for them, and re-layouts  1.31 us (4%)
  between operations  0.64 us (2%)
    pallas_call x1, Pallas kernels, shards(): pl.pallas_call(functools.partial(kernel, sizes), out_shape=(jax.ShapeDtyp...  32.7 us
    unnamed x2, local copies, waits for them, and re-layouts  1.31 us

profile of v3, /device:TPU:59, one launch (start us, length us, event | category | flops | bytes accessed | tf_op | source)
XLA Modules:
  0.0 34.6 jit_solution(14001831519288708077)
XLA Ops:
  0.6 32.7 %shard_map.104 = (f32[3,4,32,128]{3,2,1,0:T(8,128)S(1)}, f32[4,32,128]{2,1,0:T(8,128)S(1)}) custom-call(f32[3,4,32,128]{3,2,1,0:T(8,128)} %state.1, f32[2,4,32,128]{3,2,1,0:T(8,128)} %coefs.1, bf16[7,4,32,128]{3,2,1,0:T(8,128)(2,1)} %absorbers.1, s32[1,32]{1,0:T(1,128)} %bitcast.9, bf16[7,112]{1,0:T(8,128)(2,1)} %bitcast.6, f32[1,112]{1,0:T(1,128)} %bitcast.10, ...), custom_call_target="tpu_custom_call" | custom-call | tf_op jit(solution)/shard_map/pallas_call | solution.py:451
  33.3 0.7 %copy.13 = f32[3,4,32,128]{3,2,1,0:T(8,128)} copy(f32[3,4,32,128]{3,2,1,0:T(8,128)S(1)} %get-tuple-element.4) | data formatting | bytes 393216
  34.0 0.6 %copy.14 = f32[4,32,128]{2,1,0:T(8,128)} copy(f32[4,32,128]{2,1,0:T(8,128)S(1)} %get-tuple-element.5) | data formatting | bytes 131072

commit v4 on v3

--- a/solution.py
+++ b/solution.py
@@ -12,7 +12,7 @@
 H = 2 * SUB
 NDARK = 16
 PLANES = 22
-DIRECT = 14
+DIRECT = 10
 MESH = pl.DeviceIdType.MESH
 LOG2E = 1.4426950408889634
 
@@ -90,7 +90,7 @@
     route, band, solar, mass, ridx, rweight,
     wide, gas, rows_out, rows_in, sides_out, sides_in, corners_out, corners_in, exps, out, near, passing,
     p, fx, fy, bx, by, st, block_sum, sib, chip_sum, lower, part, rest, prefix, lhs, sunlit,
-    tile_sem, in_sem, send_sem, recv_sem,
+    tile_sem, in_sem, send_sem, recv_sem, ready,
 ):
     n_grp, n_gx, n_gy = sizes
     dyn_groups = 3 * n_grp // 4
@@ -118,38 +118,57 @@
         at = tall_rows * l + H
         tiles.append(pltpu.make_async_copy(state.at[:, l], wide.at[0:3, at : at + rows, :], tile_sem.at[0, l]))
         tiles.append(pltpu.make_async_copy(coefs.at[:, l], wide.at[3:5, at : at + rows, :], tile_sem.at[1, l]))
-    for load in tiles + loads:
+    for load in tiles:
         load.start()
 
-    partners = []
-    for dx, cx in ((-1, has_l), (0, None), (1, has_r)):
-        for dy, cy in ((-1, has_u), (0, None), (1, has_d)):
-            if dx == 0 and dy == 0:
-                continue
-            cond = dyn
-            if cx is not None:
-                cond = land(cond, cx)
-            if cy is not None:
-                cond = land(cond, cy)
-            partners.append((cond, {"gx": gx + dx, "gy": gy + dy}))
     seam = n_gy // 2
     far = seam >= 2
     edge_d, edge_u = land(dyn, gy == seam - 1), land(dyn, gy == seam)
-    pass_d, pass_u = land(dyn, gy == seam - 2), land(dyn, gy == seam + 1)
+    first = me < 2
+    pass_d = land(dyn, jnp.where(gy == seam - 1, me + 2 < dyn_groups, land(gy == seam - 2, first)))
+    by_way = {"grp": jnp.where(first, me, me - 2), "gy": jnp.where(first, seam - 2, seam - 1)}
+    beyond = {"grp": jnp.where(gy == seam - 1, me + 2, me), "gy": seam + 0 * gy}
+    above_us, below_us = [], []
+    for dx, cx in ((0, True), (-1, has_l), (1, has_r)):
+        here = land(dyn, cx)
+        above_us.append((land(here, has_u), {"gx": gx + dx, "gy": gy - 1}))
+        below_us.append((land(here, has_d), {"gx": gx + dx, "gy": gy + 1}))
+    aside = [
+        (land(dyn, has_r), gx + 1 <= n_gx // 2, {"gx": gx + 1}),
+        (land(dyn, has_l), gx - 1 >= n_gx // 2, {"gx": gx - 1}),
+    ]
+    same_tile = []
+    for d in sorted({1} | {2 * d for d in range(1, chips)}):
+        for other_me, cond in ((me + d, me + d < n_grp), (me - d, me - d >= 0)):
+            other_chip = lax.div(jnp.maximum(other_me, 0), 2)
+            farther = jnp.where(gy < seam, other_chip > chip, other_chip < chip)
+            late = jnp.where(other_chip == chip, core == 1, farther)
+            same_tile.append((cond, late, {"grp": other_me}))
+    beside = aside + same_tile
+    barrier = pltpu.get_barrier_semaphore()
+
+    def signal(sem, cond, dev):
+        @pl.when(cond)
+        def _():
+            pl.semaphore_signal(sem, inc=1, device_id=dev, device_id_type=MESH)
+
+    def number_of(conds):
+        return functools.reduce(lambda n, c: n + c.astype(jnp.int32), conds, jnp.int32(0))
+
+    below_late, above_late = ~edge_d, edge_u
+    for cond, dev in below_us:
+        signal(barrier, land(cond, below_late), dev)
+    for cond, dev in above_us:
+        signal(barrier, land(cond, above_late), dev)
+    for cond, late, dev in beside:
+        signal(barrier, land(cond, late), dev)
+    for load in loads:
+        load.start()
+    count = number_of([land(cond, ~late) for cond, late, _ in beside])
+    count = count + number_of([land(cond, ~above_late) for cond, _ in above_us]) + number_of([land(cond, ~below_late) for cond, _ in below_us])
     if far:
-        partners += [(pass_d, {"gy": gy + 2}), (edge_u, {"gy": gy - 2}), (pass_u, {"gy": gy - 2}), (edge_d, {"gy": gy + 2})]
-    steps = sorted({1} | {2 * d for d in range(1, chips)})
-    for d in steps:
-        partners.append((me + d < n_grp, {"grp": me + d}))
-        partners.append((me - d >= 0, {"grp": me - d}))
-    barrier = pltpu.get_barrier_semaphore()
-    count = jnp.int32(0)
-    for cond, dev in partners:
-        count = count + cond.astype(jnp.int32)
-
-        @pl.when(cond)
-        def _(dev=dev):
-            pl.semaphore_signal(barrier, inc=1, device_id=dev, device_id_type=MESH)
+        signal(barrier, edge_u, by_way)
+        count = count + pass_d.astype(jnp.int32)
 
     number = [0]
 
@@ -169,37 +188,33 @@
         return functools.reduce(land, conds)
 
     down, up = all_of(dyn, has_d), all_of(dyn, has_u)
-    halo = [
-        (down, up, remote(rows_out.at[0:DIRECT, rows - H :], rows_in.at[0, 0:DIRECT], {"gy": gy + 1})),
-        (up, down, remote(rows_out.at[0:DIRECT, 0:H], rows_in.at[1, 0:DIRECT], {"gy": gy - 1})),
-    ]
     rest_down = rows_out.at[DIRECT:PLANES, rows - H :]
     rest_up = rows_out.at[DIRECT:PLANES, 0:H]
-    down_sem, up_sem, pass_sem = number[0], number[0] + 1, number[0] + 2
+    down_sem = number[0]
     by_down = (land(down, ~edge_d) if far else down, up, remote(rest_down, rows_in.at[0, DIRECT:PLANES], {"gy": gy + 1}))
-    by_up = (land(up, ~edge_u) if far else up, down, remote(rest_up, rows_in.at[1, DIRECT:PLANES], {"gy": gy - 1}))
-    passes = []
+    to_below = [(down, up, remote(rows_out.at[0:DIRECT, rows - H :], rows_in.at[0, 0:DIRECT], {"gy": gy + 1})), by_down]
+    to_above = [
+        (up, down, remote(rows_out.at[0:DIRECT, 0:H], rows_in.at[1, 0:DIRECT], {"gy": gy - 1})),
+        (up, down, remote(rest_up, rows_in.at[1, DIRECT:PLANES], {"gy": gy - 1})),
+    ]
+    passes, relays = [], []
     if far:
-        to_pass_d = (edge_d, pass_d, remote(rest_down, passing, {"gy": gy - 1}))
-        to_pass_u = (edge_u, pass_u, remote(rest_up, passing, {"gy": gy + 1}, pass_sem))
-        passes = [to_pass_d, to_pass_u]
-    relays = []
-    if far:
-        relays = [
-            (pass_d, None, remote(passing, rows_in.at[0, DIRECT:PLANES], {"gy": gy + 2}, down_sem)),
-            (pass_u, None, remote(passing, rows_in.at[1, DIRECT:PLANES], {"gy": gy - 2}, up_sem)),
-        ]
-    halo = halo + [by_down, by_up] + [
+        passes = [(edge_d, pass_d, remote(rest_down, passing, by_way))]
+        relays = [(pass_d, None, remote(passing, rows_in.at[0, DIRECT:PLANES], beyond, down_sem))]
+    to_sides = [
         (all_of(dyn, has_r), all_of(dyn, has_l), remote(sides_out.at[0], sides_in.at[0], {"gx": gx + 1})),
         (all_of(dyn, has_l), all_of(dyn, has_r), remote(sides_out.at[1], sides_in.at[1], {"gx": gx - 1})),
     ]
     for side, (to, back, dx) in enumerate(((has_r, has_l, 1), (has_l, has_r, -1))):
         bottom = corners_out.at[side, :, rows - H :]
         top = corners_out.at[side, :, 0:H]
-        halo += [
-            (all_of(dyn, to, has_d), all_of(dyn, back, has_u), remote(bottom, corners_in.at[side, 0], {"gx": gx + dx, "gy": gy + 1})),
-            (all_of(dyn, to, has_u), all_of(dyn, back, has_d), remote(top, corners_in.at[side, 1], {"gx": gx + dx, "gy": gy - 1})),
-        ]
+        to_below.append(
+            (all_of(dyn, to, has_d), all_of(dyn, back, has_u), remote(bottom, corners_in.at[side, 0], {"gx": gx + dx, "gy": gy + 1}))
+        )
+        to_above.append(
+            (all_of(dyn, to, has_u), all_of(dyn, back, has_d), remote(top, corners_in.at[side, 1], {"gx": gx + dx, "gy": gy - 1}))
+        )
+    halo = to_below + to_above + to_sides
     half = rows // 2
     mine = pl.multiple_of(half * core, half)
     other = pl.multiple_of(half * (1 - core), half)
@@ -214,8 +229,8 @@
         (me < n_grp - 1, me > 0, remote(out.at[:, (levels - RIM) * rows : levels * rows], near.at[0], {"grp": me + 1})),
     ]
 
-    def start(item):
-        @pl.when(item[0])
+    def start(item, when=None):
+        @pl.when(item[0] if when is None else land(item[0], when))
         def _():
             item[2].start()
 
@@ -229,11 +244,48 @@
         def _():
             item[2].wait_send()
 
+    @pl.when(count > 0)
+    def _():
+        pl.semaphore_wait(barrier, count)
+
+    for cond, dev in above_us:
+        signal(ready.at[0], land(cond, ~above_late), dev)
+    for cond, dev in below_us:
+        signal(ready.at[1], land(cond, ~below_late), dev)
+    for cond, late, dev in aside:
+        signal(ready.at[2], land(cond, ~late), dev)
+    for cond, late, dev in same_tile:
+        signal(ready.at[3], land(cond, ~late), dev)
+
+    def await_ready(i, conds):
+        n = number_of(conds)
+
+        @pl.when(n > 0)
+        def _():
+            pl.semaphore_wait(ready.at[i], n)
+
     for load in tiles:
         load.wait()
 
+    exps[...] = jnp.zeros(exps.shape, jnp.float32)
+    for c in range(5):
+        for l in range(levels):
+            cells = wide[c, tall_rows * l + H : tall_rows * l + H + rows, :]
+            biggest = exponent(cells)
+            exps[levels * c + l : levels * c + l + 1, :] = biggest
+            rows_out[levels * c + l] = encode(cells, biggest)
+    for i in range(2):
+        held = exps[16 * i : 16 * i + 16, :]
+        rows_out[20 + i] = jnp.concatenate([held, held], axis=0).astype(jnp.int32).astype(jnp.int16)
+
+    for item in passes:
+        start(item)
+    for item in to_below[:2]:
+        start(item, ~below_late)
+    for item in to_above[:2]:
+        start(item, ~above_late)
+
     lane = lane_ids(rows)
-    exps[...] = jnp.zeros(exps.shape, jnp.float32)
     for q in range(3):
         right = jnp.zeros((rows, 128), jnp.float32)
         left = jnp.zeros((rows, 128), jnp.float32)
@@ -243,9 +295,6 @@
             for l in range(levels):
                 t = 2 * l + c % 2
                 cells = wide[c, tall_rows * l + H : tall_rows * l + H + rows, :]
-                biggest = exponent(cells)
-                exps[levels * c + l : levels * c + l + 1, :] = biggest
-                rows_out[levels * c + l] = encode(cells, biggest)
                 here = lax.div(lane, 16) == t
                 shift = (16 * t + 16) % 128
                 right = jnp.where(here, pltpu.roll(cells, shift, 1) if shift else cells, right)
@@ -256,12 +305,16 @@
             sides_out[side, q, 0:rows] = encode(strip, biggest)
             sides_out[side, q, rows : rows + 16] = jnp.broadcast_to(biggest, (16, 128)).astype(jnp.int32).astype(jnp.int16)
             corners_out[side, q] = strip.astype(jnp.bfloat16)
-    for i in range(2):
-        held = exps[16 * i : 16 * i + 16, :]
-        rows_out[20 + i] = jnp.concatenate([held, held], axis=0).astype(jnp.int32).astype(jnp.int16)
-
-    pl.semaphore_wait(barrier, count)
-    for item in passes + halo:
+
+    for item in to_below[2:]:
+        start(item, ~below_late)
+    for item in to_above[2:]:
+        start(item, ~above_late)
+    for item, relay in zip(passes, relays):
+        wait_recv(item)
+        start(relay)
+    await_ready(2, [land(cond, late) for cond, late, _ in aside])
+    for item in to_sides:
         start(item)
 
     loads[0].wait()
@@ -270,10 +323,12 @@
         for l in range(1, levels):
             total = total + gas[f, l].astype(jnp.float32)
         block_sum[f] = total
+    await_ready(3, [land(cond, late) for cond, late, _ in same_tile])
     to_sib.start()
-    for item, relay in zip(passes, relays):
-        wait_recv(item)
-        start(relay)
+
+    await_ready(0, [land(cond, below_late) for cond, _ in below_us])
+    for item in to_below:
+        start(item, below_late)
 
     def fill(cond, ref, *index, value=0):
         @pl.when(cond)
@@ -336,6 +391,54 @@
     for item in to_chips:
         start(item)
 
+    def radiate(start_row, ref):
+        columns = []
+        for g in range(half // 8):
+            depth = ref[:, 8 * g : 8 * g + 8, :]
+            for l in range(levels + 1):
+                if l:
+                    cells = gas[:, l - 1, pl.ds(start_row, half), :].astype(jnp.float32)
+                    depth = depth + cells[:, 8 * g : 8 * g + 8, :]
+                scaled = (depth * -LOG2E).reshape(8 * gases, 128)
+                high = scaled.astype(jnp.bfloat16).astype(jnp.float32)
+                stack = jnp.concatenate([high, scaled - high, jnp.ones((128 - 16 * gases, 128), jnp.float32)], axis=0)
+                columns.append(stack.astype(jnp.bfloat16))
+        cols = jnp.concatenate(columns, axis=1)
+        expo = jnp.dot(lhs[...], cols, preferred_element_type=jnp.float32)
+        flux = jnp.sum(jnp.exp2(expo).reshape(gpoints, 8, cols.shape[1]), axis=0)
+        for l in range(levels):
+            parts = []
+            for g in range(half // 8):
+                at = 128 * (g * (levels + 1) + l)
+                parts.append(flux[:, at : at + 128] - flux[:, at + 128 : at + 256])
+            diff = jnp.concatenate(parts, axis=0)
+            lit = sunlit[pl.ds(start_row, half), :] > 0.5
+            rate = diff / jnp.full((half, 128), mass[0, levels * me + l])
+            heating[l, pl.ds(start_row, half), :] = jnp.where(lit, rate, 0.0)
+
+    def shine():
+        for item in to_chips:
+            wait_recv(item)
+        above = jnp.zeros(rest.shape, jnp.float32)
+        for d in range(1, chips):
+            above = above + (lower[d - 1].astype(jnp.int32).astype(jnp.float32) * (1.0 / 8191.0) + 4.0)
+        even = (core == 0).astype(jnp.float32)
+        part[...] = above + even * block_sum[:, pl.ds(mine, half), :]
+        to_rest.start()
+        prefix[...] = above + (1.0 - even) * sib[...]
+        radiate(mine, prefix)
+        to_rest.wait_recv()
+        radiate(other, rest)
+
+    waits = land(gy >= seam - 1, gy <= seam)
+
+    @pl.when(waits)
+    def _():
+        shine()
+
+    await_ready(1, [land(cond, above_late) for cond, _ in above_us])
+    for item in to_above:
+        start(item, above_late)
     for item in halo:
         wait_recv(item)
 
@@ -373,44 +476,9 @@
     for item in remap:
         start(item)
 
-    for item in to_chips:
-        wait_recv(item)
-    above = jnp.zeros(rest.shape, jnp.float32)
-    for d in range(1, chips):
-        above = above + (lower[d - 1].astype(jnp.int32).astype(jnp.float32) * (1.0 / 8191.0) + 4.0)
-    even = (core == 0).astype(jnp.float32)
-    part[...] = above + even * block_sum[:, pl.ds(mine, half), :]
-    to_rest.start()
-    prefix[...] = above + (1.0 - even) * sib[...]
-
-    def radiate(start_row, ref):
-        columns = []
-        for g in range(half // 8):
-            depth = ref[:, 8 * g : 8 * g + 8, :]
-            for l in range(levels + 1):
-                if l:
-                    cells = gas[:, l - 1, pl.ds(start_row, half), :].astype(jnp.float32)
-                    depth = depth + cells[:, 8 * g : 8 * g + 8, :]
-                scaled = (depth * -LOG2E).reshape(8 * gases, 128)
-                high = scaled.astype(jnp.bfloat16).astype(jnp.float32)
-                stack = jnp.concatenate([high, scaled - high, jnp.ones((128 - 16 * gases, 128), jnp.float32)], axis=0)
-                columns.append(stack.astype(jnp.bfloat16))
-        cols = jnp.concatenate(columns, axis=1)
-        expo = jnp.dot(lhs[...], cols, preferred_element_type=jnp.float32)
-        flux = jnp.sum(jnp.exp2(expo).reshape(gpoints, 8, cols.shape[1]), axis=0)
-        for l in range(levels):
-            parts = []
-            for g in range(half // 8):
-                at = 128 * (g * (levels + 1) + l)
-                parts.append(flux[:, at : at + 128] - flux[:, at + 128 : at + 256])
-            diff = jnp.concatenate(parts, axis=0)
-            lit = sunlit[pl.ds(start_row, half), :] > 0.5
-            rate = diff / jnp.full((half, 128), mass[0, levels * me + l])
-            heating[l, pl.ds(start_row, half), :] = jnp.where(lit, rate, 0.0)
-
-    radiate(mine, prefix)
-    to_rest.wait_recv()
-    radiate(other, rest)
+    @pl.when(~waits)
+    def _():
+        shine()
 
     for item in remap:
         wait_recv(item)
@@ -486,6 +554,7 @@
             pltpu.SemaphoreType.DMA((7,)),
             pltpu.SemaphoreType.DMA((n_copies,)),
             pltpu.SemaphoreType.DMA((n_copies,)),
+            pltpu.SemaphoreType.REGULAR((4,)),
         ],
         compiler_params=pltpu.CompilerParams(collective_id=0, has_side_effects=True, vmem_limit_bytes=40 * 2**20),
     )(

time: 34.8 us -> 33.2 us (0.954)
  Pallas kernels: 32.7 us -> 31.1 us
    pallas_call x1, Pallas kernels: 32.7 us -> 31.1 us  [shards(): pl.pallas_call(functools.partial(kernel, sizes), out_shape=(jax.ShapeDtyp...]
where the time goes in v4:
time: 33.2 us; the launch traced here: 33.1 us
  Pallas kernels  31.1 us (94%)
  local copies, waits for them, and re-layouts  1.31 us (4%)
  between operations  0.64 us (2%)
    pallas_call x1, Pallas kernels, shards(): pl.pallas_call(functools.partial(kernel, sizes), out_shape=(jax.ShapeDtyp...  31.1 us
    unnamed x2, local copies, waits for them, and re-layouts  1.31 us

profile of v4, /device:TPU:59, one launch (start us, length us, event | category | flops | bytes accessed | tf_op | source)
XLA Modules:
  0.0 33.1 jit_solution(12747222777896845832)
XLA Ops:
  0.6 31.1 %shard_map.104 = (f32[3,4,32,128]{3,2,1,0:T(8,128)S(1)}, f32[4,32,128]{2,1,0:T(8,128)S(1)}) custom-call(f32[3,4,32,128]{3,2,1,0:T(8,128)} %state.1, f32[2,4,32,128]{3,2,1,0:T(8,128)} %coefs.1, bf16[7,4,32,128]{3,2,1,0:T(8,128)(2,1)} %absorbers.1, s32[1,32]{1,0:T(1,128)} %bitcast.9, bf16[7,112]{1,0:T(8,128)(2,1)} %bitcast.6, f32[1,112]{1,0:T(1,128)} %bitcast.10, ...), custom_call_target="tpu_custom_call" | custom-call | tf_op jit(solution)/shard_map/pallas_call | solution.py:519
  31.7 0.7 %copy.13 = f32[3,4,32,128]{3,2,1,0:T(8,128)} copy(f32[3,4,32,128]{3,2,1,0:T(8,128)S(1)} %get-tuple-element.4) | data formatting | bytes 393216
  32.4 0.6 %copy.14 = f32[4,32,128]{2,1,0:T(8,128)} copy(f32[4,32,128]{2,1,0:T(8,128)S(1)} %get-tuple-element.5) | data formatting | bytes 131072

commit v5 on v4

--- a/solution.py
+++ b/solution.py
@@ -46,11 +46,12 @@
     return [(i, min(i + size, stop)) for i in range(start, stop, size)]
 
 
-def substeps(wide, p, fx, fy, bx, by, st, out):
-    rows = wide.shape[1] // 8
+def substeps(wide, base, p, fx, fy, bx, by, st, out):
+    rows = p.shape[0]
+    tall_rows = wide.shape[1] // 8
 
     def row(c, r):
-        return wide[c, pl.ds(r, 8, stride=rows), :]
+        return wide[c, pl.ds(base + r, 8, stride=tall_rows), :]
 
     for i, j in chunks(0, rows):
         for r in range(i, j):
@@ -225,8 +226,11 @@
     ]
     to_rest = remote(part, rest, sibling)
     remap = [
-        (me > 0, me < n_grp - 1, remote(out.at[:, 0 : RIM * rows], near.at[1], {"grp": me - 1})),
-        (me < n_grp - 1, me > 0, remote(out.at[:, (levels - RIM) * rows : levels * rows], near.at[0], {"grp": me + 1})),
+        [
+            (me > 0, me < n_grp - 1, remote(out.at[h, :, 0 : RIM * half], near.at[1, h], {"grp": me - 1})),
+            (me < n_grp - 1, me > 0, remote(out.at[h, :, (levels - RIM) * half : levels * half], near.at[0, h], {"grp": me + 1})),
+        ]
+        for h in range(2)
     ]
 
     def start(item, when=None):
@@ -353,7 +357,9 @@
     def _():
         for c in range(3):
             for l in range(levels):
-                out[c, rows * l : rows * l + rows, :] = wide[c, tall_rows * l + H : tall_rows * l + H + rows, :]
+                for h in range(2):
+                    at = tall_rows * l + H + half * h
+                    out[h, c, half * l : half * l + half, :] = wide[c, at : at + half, :]
 
     for load in loads[1:]:
         load.wait()
@@ -436,70 +442,95 @@
     def _():
         shine()
 
-    await_ready(1, [land(cond, above_late) for cond, _ in above_us])
-    for item in to_above:
-        start(item, above_late)
-    for item in halo:
+    lane_h = lane_ids(rows + H)
+
+    def decode_rows(i, at):
+        exps[...] = jnp.concatenate([rows_in[i, 20], rows_in[i, 21]], axis=0).astype(jnp.int32).astype(jnp.float32)
+        for c in range(5):
+            for l in range(levels):
+                k = levels * c + l
+                wide[c, tall_rows * l + at : tall_rows * l + at + H, :] = decode(rows_in[i, k], exps[k : k + 1, :])
+
+    def place_sides(q, strips, at):
+        n = strips[0].shape[0]
+        for c in (2 * q, 2 * q + 1):
+            if c > 4:
+                continue
+            for l in range(levels):
+                t = 2 * l + c % 2
+                shift = (112 - 16 * t) % 128
+                left = pltpu.roll(strips[0], shift, 1) if shift else strips[0]
+                shift = (128 - 16 * t) % 128
+                right = pltpu.roll(strips[1], shift, 1) if shift else strips[1]
+                start_row = tall_rows * (levels + l) + at
+                wide[c, start_row : start_row + n, :] = jnp.where(
+                    lane_h[0:n] < 16, right, jnp.where(lane_h[0:n] >= 112, left, 0.0)
+                )
+
+    for item in to_above + to_sides:
         wait_recv(item)
 
     @pl.when(dyn)
     def _():
-        for i, at in enumerate((0, H + rows)):
-            biggest = jnp.concatenate([rows_in[i, 20], rows_in[i, 21]], axis=0).astype(jnp.int32).astype(jnp.float32)
-            exps[...] = biggest
-            for c in range(5):
-                for l in range(levels):
-                    k = levels * c + l
-                    wide[c, tall_rows * l + at : tall_rows * l + at + H, :] = decode(rows_in[i, k], exps[k : k + 1, :])
-        lane_w = lane_ids(rows + 2 * H)
+        decode_rows(1, H + rows)
         for q in range(3):
             strips = []
             for side in range(2):
                 biggest = sides_in[side, q, rows : rows + 16].astype(jnp.int32).astype(jnp.float32)[0:1]
                 middle = decode(sides_in[side, q, 0:rows], biggest)
-                ends = [corners_in[side, i, q].astype(jnp.float32) for i in range(2)]
-                strips.append(jnp.concatenate([ends[0], middle, ends[1]], axis=0))
-            for c in (2 * q, 2 * q + 1):
-                if c > 4:
-                    continue
-                for l in range(levels):
-                    t = 2 * l + c % 2
-                    shift = (112 - 16 * t) % 128
-                    left = pltpu.roll(strips[0], shift, 1) if shift else strips[0]
-                    shift = (128 - 16 * t) % 128
-                    right = pltpu.roll(strips[1], shift, 1) if shift else strips[1]
-                    wide[c, tall_rows * (levels + l) : tall_rows * (levels + l + 1), :] = jnp.where(
-                        lane_w < 16, right, jnp.where(lane_w >= 112, left, 0.0)
-                    )
-        substeps(wide, p, fx, fy, bx, by, st, out)
-
-    for item in remap:
+                strips.append(jnp.concatenate([middle, corners_in[side, 1, q].astype(jnp.float32)], axis=0))
+            place_sides(q, strips, H)
+        substeps(wide, half, p, fx, fy, bx, by, st, out.at[1])
+
+    for item in remap[1]:
+        start(item)
+    await_ready(1, [land(cond, above_late) for cond, _ in above_us])
+    for item in to_above:
+        start(item, above_late)
+
+    for item in to_below:
+        wait_recv(item)
+
+    @pl.when(dyn)
+    def _():
+        decode_rows(0, 0)
+        for q in range(3):
+            place_sides(q, [corners_in[side, 0, q].astype(jnp.float32) for side in range(2)], 0)
+        substeps(wide, 0, p, fx, fy, bx, by, st, out.at[0])
+
+    for item in remap[0]:
         start(item)
 
     @pl.when(~waits)
     def _():
         shine()
 
-    for item in remap:
-        wait_recv(item)
+    weights = []
     for kl in range(levels):
         k = levels * me + kl
-        weights = []
         for o in range(-RIM, RIM + 1):
             w = jnp.float32(0)
             for j in range(ridx.shape[0]):
                 w = w + jnp.where(ridx[j, k] == k + o, rweight[j, k], jnp.float32(0))
             weights.append(w)
-        for c in range(3):
-            acc = jnp.zeros((rows, 128), jnp.float32)
-            for o in range(-RIM, RIM + 1):
-                m = kl + o
-                ref, m = (near.at[0], m + RIM) if m < 0 else (out, m) if m < levels else (near.at[1], m - levels)
-                cells = ref[c, rows * m : rows * m + rows, :]
-                acc = acc + weights[o + RIM] * cells
-            new_state[c, kl] = acc
-
-    for item in passes + relays + halo + to_chips + remap:
+    for h in (1, 0):
+        for item in remap[h]:
+            wait_recv(item)
+        for kl in range(levels):
+            for c in range(3):
+                acc = jnp.zeros((half, 128), jnp.float32)
+                for o in range(-RIM, RIM + 1):
+                    m = kl + o
+                    if m < 0:
+                        cells = near[0, h, c, half * (m + RIM) : half * (m + RIM + 1), :]
+                    elif m < levels:
+                        cells = out[h, c, half * m : half * m + half, :]
+                    else:
+                        cells = near[1, h, c, half * (m - levels) : half * (m - levels + 1), :]
+                    acc = acc + weights[(2 * RIM + 1) * kl + o + RIM] * cells
+                new_state[c, kl, half * h : half * h + half, :] = acc
+
+    for item in passes + relays + halo + to_chips + remap[0] + remap[1]:
         wait_send(item)
     to_sib.wait_send()
     to_rest.wait_send()
@@ -515,7 +546,7 @@
         state, coefs, lagged_absorbers, sun_route.T, band_coef.T, solar.reshape(1, -1), layer_mass.reshape(1, -1),
         remap_index.T, remap_weight.T,
     )
-    n_copies = 14 + 1 + (chips - 1) + 1 + 2
+    n_copies = 16 + 1 + (chips - 1) + 1 + 2
     return pl.pallas_call(
         functools.partial(kernel, sizes),
         out_shape=(jax.ShapeDtypeStruct(state.shape, f32), jax.ShapeDtypeStruct(state.shape[1:], f32)),
@@ -537,10 +568,10 @@
             pltpu.VMEM((2, 3, rows, 128), bf16),
             pltpu.VMEM((2, 2, 3, H, 128), bf16),
             pltpu.VMEM((32, 128), f32),
-            pltpu.VMEM((3, 2 * levels * rows, 128), f32),
-            pltpu.VMEM((2, 3, RIM * rows, 128), f32),
+            pltpu.VMEM((2, 3, levels * rows, 128), f32),
+            pltpu.VMEM((2, 2, 3, RIM * rows // 2, 128), f32),
             pltpu.VMEM((PLANES - DIRECT, H, 128), i16),
-            *[pltpu.VMEM((rows + 2 * H, 2 * levels, 128), f32)] * 6,
+            *[pltpu.VMEM((rows // 2 + 2 * H, 2 * levels, 128), f32)] * 6,
             pltpu.VMEM((gases, rows, 128), f32),
             pltpu.VMEM((gases, rows // 2, 128), f32),
             pltpu.VMEM((gases, rows // 2, 128), i16),

time: 33.2 us -> 32 us (0.964)
  Pallas kernels: 31.1 us -> 29.9 us
    pallas_call x1, Pallas kernels: 31.1 us -> 29.9 us  [shards(): pl.pallas_call(functools.partial(kernel, sizes), out_shape=(jax.ShapeDtyp...]
where the time goes in v5:
time: 32 us; the launch traced here: 31.8 us
  Pallas kernels  29.9 us (93%)
  local copies, waits for them, and re-layouts  1.31 us (4%)
  between operations  0.64 us (2%)
    pallas_call x1, Pallas kernels, shards(): pl.pallas_call(functools.partial(kernel, sizes), out_shape=(jax.ShapeDtyp...  29.9 us
    unnamed x2, local copies, waits for them, and re-layouts  1.31 us

profile of v5, /device:TPU:59, one launch (start us, length us, event | category | flops | bytes accessed | tf_op | source)
XLA Modules:
  0.0 31.8 jit_solution(14994193904989892349)
XLA Ops:
  0.6 29.9 %shard_map.104 = (f32[3,4,32,128]{3,2,1,0:T(8,128)S(1)}, f32[4,32,128]{2,1,0:T(8,128)S(1)}) custom-call(f32[3,4,32,128]{3,2,1,0:T(8,128)} %state.1, f32[2,4,32,128]{3,2,1,0:T(8,128)} %coefs.1, bf16[7,4,32,128]{3,2,1,0:T(8,128)(2,1)} %absorbers.1, s32[1,32]{1,0:T(1,128)} %bitcast.9, bf16[7,112]{1,0:T(8,128)(2,1)} %bitcast.6, f32[1,112]{1,0:T(1,128)} %bitcast.10, ...), custom_call_target="tpu_custom_call" | custom-call | tf_op jit(solution)/shard_map/pallas_call | solution.py:550
  30.5 0.7 %copy.13 = f32[3,4,32,128]{3,2,1,0:T(8,128)} copy(f32[3,4,32,128]{3,2,1,0:T(8,128)S(1)} %get-tuple-element.4) | data formatting | bytes 393216
  31.2 0.6 %copy.14 = f32[4,32,128]{2,1,0:T(8,128)} copy(f32[4,32,128]{2,1,0:T(8,128)S(1)} %get-tuple-element.5) | data formatting | bytes 131072

commit v6 on v5

--- a/solution.py
+++ b/solution.py
@@ -46,24 +46,25 @@
     return [(i, min(i + size, stop)) for i in range(start, stop, size)]
 
 
-def substeps(wide, base, p, fx, fy, bx, by, st, out):
-    rows = p.shape[0]
+def prepare(wide, base, start, stop, p, fx, fy, bx, by, st):
     tall_rows = wide.shape[1] // 8
 
     def row(c, r):
         return wide[c, pl.ds(base + r, 8, stride=tall_rows), :]
 
-    for i, j in chunks(0, rows):
+    for i, j in chunks(start, stop):
         for r in range(i, j):
             p[r] = row(2, r)
             st[r] = row(4, r)
-            fy[r] = row(1, r)
-            by[r] = row(3, r)
             if r > 0:
                 fx[r - 1] = row(0, r)
-                bx[r - 1] = by[r]
-        fy[i:j] = turned(fy[i:j], -1)
-        by[i:j] = turned(by[i:j], -1)
+                bx[r - 1] = row(3, r)
+        fy[i:j] = turned(jnp.stack([row(1, r) for r in range(i, j)]), -1)
+        by[i:j] = turned(jnp.stack([row(3, r) for r in range(i, j)]), -1)
+
+
+def substeps(p, fx, fy, bx, by, st, out):
+    rows = p.shape[0]
     first = 0
     pv, xv, yv = p[...], fx[0 : rows - 1], fy[...]
     for step in range(SUB):
@@ -268,12 +269,12 @@
         def _():
             pl.semaphore_wait(ready.at[i], n)
 
-    for load in tiles:
-        load.wait()
 
     exps[...] = jnp.zeros(exps.shape, jnp.float32)
-    for c in range(5):
-        for l in range(levels):
+    for l in range(levels):
+        for load in tiles[2 * l : 2 * l + 2]:
+            load.wait()
+        for c in range(5):
             cells = wide[c, tall_rows * l + H : tall_rows * l + H + rows, :]
             biggest = exponent(cells)
             exps[levels * c + l : levels * c + l + 1, :] = biggest
@@ -480,7 +481,8 @@
                 middle = decode(sides_in[side, q, 0:rows], biggest)
                 strips.append(jnp.concatenate([middle, corners_in[side, 1, q].astype(jnp.float32)], axis=0))
             place_sides(q, strips, H)
-        substeps(wide, half, p, fx, fy, bx, by, st, out.at[1])
+        prepare(wide, half, 0, half + 2 * H, p, fx, fy, bx, by, st)
+        substeps(p, fx, fy, bx, by, st, out.at[1])
 
     for item in remap[1]:
         start(item)
@@ -488,6 +490,10 @@
     for item in to_above:
         start(item, above_late)
 
+    @pl.when(dyn)
+    def _():
+        prepare(wide, 0, H, half + 2 * H, p, fx, fy, bx, by, st)
+
     for item in to_below:
         wait_recv(item)
 
@@ -496,7 +502,8 @@
         decode_rows(0, 0)
         for q in range(3):
             place_sides(q, [corners_in[side, 0, q].astype(jnp.float32) for side in range(2)], 0)
-        substeps(wide, 0, p, fx, fy, bx, by, st, out.at[0])
+        prepare(wide, 0, 0, H, p, fx, fy, bx, by, st)
+        substeps(p, fx, fy, bx, by, st, out.at[0])
 
     for item in remap[0]:
         start(item)

time: 32 us -> 31.7 us (level)
  no operation moved by 1% of the time
where the time goes in v6:
time: 31.7 us; the launch traced here: 31.5 us
  Pallas kernels  29.6 us (93%)
  local copies, waits for them, and re-layouts  1.31 us (4%)
  between operations  0.64 us (2%)
    pallas_call x1, Pallas kernels, shards(): pl.pallas_call(functools.partial(kernel, sizes), out_shape=(jax.ShapeDtyp...  29.6 us
    unnamed x2, local copies, waits for them, and re-layouts  1.31 us

profile of v6, /device:TPU:59, one launch (start us, length us, event | category | flops | bytes accessed | tf_op | source)
XLA Modules:
  0.0 31.5 jit_solution(13637325815980118518)
XLA Ops:
  0.6 29.6 %shard_map.104 = (f32[3,4,32,128]{3,2,1,0:T(8,128)S(1)}, f32[4,32,128]{2,1,0:T(8,128)S(1)}) custom-call(f32[3,4,32,128]{3,2,1,0:T(8,128)} %state.1, f32[2,4,32,128]{3,2,1,0:T(8,128)} %coefs.1, bf16[7,4,32,128]{3,2,1,0:T(8,128)(2,1)} %absorbers.1, s32[1,32]{1,0:T(1,128)} %bitcast.9, bf16[7,112]{1,0:T(8,128)(2,1)} %bitcast.6, f32[1,112]{1,0:T(1,128)} %bitcast.10, ...), custom_call_target="tpu_custom_call" | custom-call | tf_op jit(solution)/shard_map/pallas_call | solution.py:557
  30.2 0.7 %copy.13 = f32[3,4,32,128]{3,2,1,0:T(8,128)} copy(f32[3,4,32,128]{3,2,1,0:T(8,128)S(1)} %get-tuple-element.4) | data formatting | bytes 393216
  30.9 0.6 %copy.14 = f32[4,32,128]{2,1,0:T(8,128)} copy(f32[4,32,128]{2,1,0:T(8,128)S(1)} %get-tuple-element.5) | data formatting | bytes 131072

commit v7 on v6

--- a/solution.py
+++ b/solution.py
@@ -468,6 +468,11 @@
                     lane_h[0:n] < 16, right, jnp.where(lane_h[0:n] >= 112, left, 0.0)
                 )
 
+    def send_levels(pair):
+        start(pair[0], core == 0)
+        start(pair[1])
+        start(pair[0], core == 1)
+
     for item in to_above + to_sides:
         wait_recv(item)
 
@@ -484,8 +489,7 @@
         prepare(wide, half, 0, half + 2 * H, p, fx, fy, bx, by, st)
         substeps(p, fx, fy, bx, by, st, out.at[1])
 
-    for item in remap[1]:
-        start(item)
+    send_levels(remap[1])
     await_ready(1, [land(cond, above_late) for cond, _ in above_us])
     for item in to_above:
         start(item, above_late)
@@ -505,8 +509,7 @@
         prepare(wide, 0, 0, H, p, fx, fy, bx, by, st)
         substeps(p, fx, fy, bx, by, st, out.at[0])
 
-    for item in remap[0]:
-        start(item)
+    send_levels(remap[0])
 
     @pl.when(~waits)
     def _():

time: 31.7 us -> 31.7 us (level)
  no operation moved by 1% of the time
where the time goes in v7:
time: 31.7 us; the launch traced here: 31.5 us
  Pallas kernels  29.6 us (93%)
  local copies, waits for them, and re-layouts  1.31 us (4%)
  between operations  0.64 us (2%)
    pallas_call x1, Pallas kernels, shards(): pl.pallas_call(functools.partial(kernel, sizes), out_shape=(jax.ShapeDtyp...  29.6 us
    unnamed x2, local copies, waits for them, and re-layouts  1.31 us

profile of v7, /device:TPU:59, one launch (start us, length us, event | category | flops | bytes accessed | tf_op | source)
XLA Modules:
  0.0 31.5 jit_solution(6998544623738352063)
XLA Ops:
  0.6 29.6 %shard_map.104 = (f32[3,4,32,128]{3,2,1,0:T(8,128)S(1)}, f32[4,32,128]{2,1,0:T(8,128)S(1)}) custom-call(f32[3,4,32,128]{3,2,1,0:T(8,128)} %state.1, f32[2,4,32,128]{3,2,1,0:T(8,128)} %coefs.1, bf16[7,4,32,128]{3,2,1,0:T(8,128)(2,1)} %absorbers.1, s32[1,32]{1,0:T(1,128)} %bitcast.9, bf16[7,112]{1,0:T(8,128)(2,1)} %bitcast.6, f32[1,112]{1,0:T(1,128)} %bitcast.10, ...), custom_call_target="tpu_custom_call" | custom-call | tf_op jit(solution)/shard_map/pallas_call | solution.py:560
  30.2 0.7 %copy.13 = f32[3,4,32,128]{3,2,1,0:T(8,128)} copy(f32[3,4,32,128]{3,2,1,0:T(8,128)S(1)} %get-tuple-element.4) | data formatting | bytes 393216
  30.9 0.6 %copy.14 = f32[4,32,128]{2,1,0:T(8,128)} copy(f32[4,32,128]{2,1,0:T(8,128)S(1)} %get-tuple-element.5) | data formatting | bytes 131072
